TPU v7x, 256 devices: a whole 4x4x8 slice. The times are simulated.
256 devices in a mesh: row: 16 (over z, x_lo), col: 16 (over y, x_hi, core).
Axes of the slice: x: 4 (x_hi: 2, x_lo: 2; x = x_hi * 2 + x_lo), y: 4, z: 8, core: 2. Of those that a mesh axis runs over, the one named last changes fastest.
Arguments:
- tiles: bfloat16 [16, 16, 320, 128, 128], P('row', 'col'), may hold values from 0 to 0.099609375
- tile_rows: int32 [16, 16, 320], P('row', 'col'), may hold values from 0 to 63
- tile_cols: int32 [16, 16, 320], P('row', 'col'), may hold values from 0 to 63
- node_level: int32 [131072], P(('row', 'col')), may hold values from 0 to 127
- level_scale: float32 [128], replicated, may hold values from 0.15 to 1.5
- stored_basis: bfloat16 [131072, 64], P(('row', 'col')), may hold values from -20 to 20
- start_block: bfloat16 [131072, 32], P(('row', 'col')), may hold values from -33 to 33
Outputs:
- first_block: bfloat16 [131072, 32], P(('row', 'col'))
- second_block: bfloat16 [131072, 32], P(('row', 'col'))
All inputs are finite; a program needn't handle non-finite values.
Results may differ from a plain program's by a relative error of at most 0.02.
Values may be sent and summed in bfloat16 or wider, within the bound.
No kernel may reach another device: no remote copies, remote signals or barrier semaphores. Data moves between devices by JAX's collectives and lax.ppermute only.
A program may use at most 64 MiB of HBM per device.

v0:
```python
import jax
import jax.numpy as jnp
from jax import lax
from jax.sharding import PartitionSpec as P


def solve_gram(gram_matrix, right_side):
    factor = jnp.linalg.cholesky(gram_matrix)
    partway = lax.linalg.triangular_solve(factor, right_side, left_side=True, lower=True)
    return lax.linalg.triangular_solve(
        factor, partway, left_side=True, lower=True, transpose_a=True
    )


def normalize(remainder, squares):
    factor = jnp.linalg.cholesky(squares)
    return lax.linalg.triangular_solve(
        factor, remainder, left_side=False, lower=True, transpose_a=True
    )


def similarity(vectors, node_scale, tile_stack, rows_index, cols_index):
    columns = vectors.shape[1]
    tile_edge = tile_stack.shape[-1]
    scaled = (node_scale[:, None] * vectors.astype(jnp.float32)).astype(jnp.bfloat16)
    packed = scaled.reshape(-1, 128)
    column_block = lax.all_gather(packed, "row", axis=0, tiled=True).reshape(-1, tile_edge, columns)
    row_block = lax.all_gather(packed, "col", axis=0, tiled=True).reshape(-1, tile_edge, columns)
    forward_terms = jnp.einsum(
        "tij,tjk->tik", tile_stack, column_block[cols_index], preferred_element_type=jnp.float32
    )
    backward_terms = jnp.einsum(
        "tji,tjk->tik", tile_stack, row_block[rows_index], preferred_element_type=jnp.float32
    )
    forward_rows = jnp.zeros(row_block.shape, jnp.float32).at[rows_index].add(forward_terms)
    own_forward = lax.psum_scatter(
        forward_rows.reshape(-1, 128), "col", scatter_dimension=0, tiled=True
    ).reshape(-1, columns)
    backward_cols = jnp.zeros(column_block.shape, jnp.float32).at[cols_index].add(backward_terms)
    own_backward = lax.psum_scatter(
        backward_cols.reshape(-1, 128), "row", scatter_dimension=0, tiled=True
    ).reshape(-1, columns)
    total = scaled.astype(jnp.float32) + own_forward + own_backward
    return (node_scale[:, None] * total).astype(jnp.bfloat16)


def extend(basis, known, image, nodes):
    kept_count = known.shape[0]
    newest = basis[:, kept_count:]
    fresh = newest.shape[1]
    paired = jnp.concatenate([newest, image], axis=1)
    local_part = jnp.einsum("nk,nj->kj", basis, paired, preferred_element_type=jnp.float32)
    summed = lax.psum(local_part, ("row", "col"))
    upper = jnp.concatenate([known, summed[:kept_count, :fresh]], axis=1)
    gram_matrix = jnp.concatenate([upper, summed[:, :fresh].T], axis=0)
    cross = summed[:, fresh:]
    coefficients = solve_gram(gram_matrix, cross).astype(jnp.bfloat16)
    remainder = image.astype(jnp.float32) - jnp.dot(
        basis, coefficients, preferred_element_type=jnp.float32
    )
    local_rem = jnp.dot(remainder.T, remainder, precision=lax.Precision.HIGHEST)
    squares = lax.psum(local_rem, ("row", "col")) / nodes
    return (normalize(remainder, squares).astype(jnp.bfloat16), gram_matrix)


def per_device(tiles, tile_rows, tile_cols, node_level, level_scale, stored_basis, start_block):
    tile_stack = tiles.reshape(tiles.shape[2:])
    rows_index = tile_rows.reshape(-1)
    cols_index = tile_cols.reshape(-1)
    member = node_level[:, None] == jnp.arange(level_scale.shape[0], dtype=jnp.int32)[None, :]
    node_scale = jnp.sum(jnp.where(member, level_scale[None, :], 0.0), axis=1)
    nodes = stored_basis.shape[0] * lax.axis_size("row") * lax.axis_size("col")
    first_basis = jnp.concatenate([stored_basis, start_block], axis=1)
    image = similarity(start_block, node_scale, tile_stack, rows_index, cols_index)
    first_block, first_gram = extend(first_basis, jnp.zeros((0, 0), jnp.float32), image, nodes)
    second_basis = jnp.concatenate([first_basis, first_block], axis=1)
    image = similarity(first_block, node_scale, tile_stack, rows_index, cols_index)
    second_block, second_gram = extend(second_basis, first_gram, image, nodes)
    return (first_block, second_block)


def solution(mesh):
    return jax.shard_map(
        per_device,
        mesh=mesh,
        in_specs=(
            P("row", "col", None, None, None),
            P("row", "col", None),
            P("row", "col", None),
            P(("row", "col")),
            P(),
            P(("row", "col"), None),
            P(("row", "col"), None),
        ),
        out_specs=(P(("row", "col"), None), P(("row", "col"), None)),
        check_vma=False,
    )
```

profile of v0, /device:TPU:4, one launch (start us, length us, event | category | flops | bytes accessed | tf_op | source)
XLA Modules:
  0.0 833.3 jit_solution(2884602566155082557)
XLA Ops:
  9.2 39.1 %all_gather.12 = bf16[2048,128]{1,0:T(8,128)(2,1)S(1)} all-gather(bf16[128,128]{1,0:T(8,128)(2,1)S(1)} %reshape.147), channel_id=1, replica_groups=mesh['row'=16,'col'=16] {'row'}, dimensions={0}, use_global_device_ids=true | all-gather | bytes 557056 | tf_op jit(solution)/shard_map/all_gather | solution.py:27
  52.4 9.7 %fusion.8 = f32[320,128,32]{1,2,0:T(8,128)} fusion(bf16[320,128,32]{1,2,0:T(8,128)(2,1)S(1)} %gather_fusion, bf16[1,1,320,128,128]{4,3,2,1,0:T(8,128)(2,1)} %param.10), kind=kOutput, calls=%fused_computation.16 | convolution fusion | flops 335544320 | bytes 18350080 | tf_op jit(solution)/shard_map/tij,tjk->tik/dot_general | solution.py:29
  62.3 28.7 %scatter_fusion = f32[64,128,32]{1,2,0:T(8,128)S(1)} fusion(f32[64,128,32]{1,2,0:T(8,128)S(1)} %broadcast.195.clone.1, s32[320]{0:T(512)S(1)} %fusion.46, f32[320,128,32]{1,2,0:T(8,128)} %fusion.8), kind=kCustom, calls=%fused_computation.4 | custom fusion | flops 1310720 | bytes 15729920 | tf_op jit(solution)/shard_map/scatter-add | solution.py:35
  93.6 4.1 reshape.151
  97.8 21.8 %all_gather.13 = bf16[2048,128]{1,0:T(8,128)(2,1)S(1)} all-gather(bf16[128,128]{1,0:T(8,128)(2,1)S(1)} %reshape.147), channel_id=1, replica_groups=mesh['row'=16,'col'=16] {'col'}, dimensions={0}, use_global_device_ids=true | all-gather | bytes 557056 | tf_op jit(solution)/shard_map/all_gather | solution.py:28
  123.6 7.1 fusion.11
  130.8 28.7 %scatter_fusion.1 = f32[64,128,32]{1,2,0:T(8,128)S(1)} fusion(f32[64,128,32]{1,2,0:T(8,128)S(1)} %broadcast.195.clone, s32[320]{0:T(512)S(1)} %fusion.47, f32[320,128,32]{1,2,0:T(8,128)} %fusion.11), kind=kCustom, calls=%fused_computation.5 | custom fusion | flops 1310720 | bytes 15729920 | tf_op jit(solution)/shard_map/scatter-add | solution.py:39
  159.6 2.6 copy.48
  162.2 4.1 reshape.154
  166.5 2.9 reduce-scatter.5.cloned.1.call-done
  170.4 72.8 %reduce-scatter.7.cloned.1.call-done = f32[128,128]{1,0:T(8,128)} async-done(((f32[2048,128]{1,0:T(8,128)}), f32[128,128]{1,0:T(8,128)}) %reduce-scatter.7.cloned.1.call-update) | async-done | bytes 65552 | tf_op jit(solution)/shard_map/reduce_scatter | solution.py:40
  244.5 73.1 %psum.28 = f32[96,128]{0,1:T(8,128)S(1)} all-reduce(f32[96,128]{0,1:T(8,128)S(1)} %fusion.22), channel_id=1, replica_groups=mesh['row'=16,'col'=16] {'row','col'}, use_global_device_ids=true, to_apply=%region_5.6 | all-reduce | flops 12288 | bytes 98304 | tf_op jit(solution)/shard_map/psum | solution.py:53
  317.7 8.8 %cholesky.56 = f32[96,96]{1,0:T(8,128)S(1)} custom-call(f32[96,96]{1,0:T(8,128)S(1)} %copy.52), custom_call_target="Cholesky" | custom-call | tf_op jit(solution)/shard_map/jit(cholesky)/cholesky | solution.py:8
  327.9 7.4 custom-call.21
  335.9 73.5 %psum.29 = f32[32,32]{0,1:T(8,128)S(1)} all-reduce(f32[32,32]{0,1:T(8,128)S(1)} %fusion.51), channel_id=1, replica_groups=mesh['row'=16,'col'=16] {'row','col'}, use_global_device_ids=true, to_apply=%region_8.9 | all-reduce | flops 1024 | bytes 8192 | tf_op jit(solution)/shard_map/psum | solution.py:62
  409.5 2.9 cholesky.114
  416.7 36.8 %all_gather.14 = bf16[2048,128]{1,0:T(8,128)(2,1)S(1)} all-gather(bf16[128,128]{1,0:T(8,128)(2,1)S(1)} %reshape.156), channel_id=1, replica_groups=mesh['row'=16,'col'=16] {'row'}, dimensions={0}, use_global_device_ids=true | all-gather | bytes 557056 | tf_op jit(solution)/shard_map/all_gather | solution.py:27
  457.6 9.7 %fusion.14 = f32[320,128,32]{1,2,0:T(8,128)} fusion(bf16[320,128,32]{1,2,0:T(8,128)(2,1)S(1)} %gather_fusion.2, bf16[1,1,320,128,128]{4,3,2,1,0:T(8,128)(2,1)} %param.10), kind=kOutput, calls=%fused_computation.18 | convolution fusion | flops 335544320 | bytes 18350080 | tf_op jit(solution)/shard_map/tij,tjk->tik/dot_general | solution.py:29
  467.5 28.7 %scatter_fusion.2 = f32[64,128,32]{1,2,0:T(8,128)S(1)} fusion(f32[64,128,32]{1,2,0:T(8,128)S(1)} %broadcast.195.clone.3, s32[320]{0:T(512)S(1)} %fusion.46, f32[320,128,32]{1,2,0:T(8,128)} %fusion.14), kind=kCustom, calls=%fused_computation.6 | custom fusion | flops 1310720 | bytes 15729920 | tf_op jit(solution)/shard_map/scatter-add | solution.py:35
  498.8 4.1 reshape.158
  503.0 21.4 %all_gather.15 = bf16[2048,128]{1,0:T(8,128)(2,1)S(1)} all-gather(bf16[128,128]{1,0:T(8,128)(2,1)S(1)} %reshape.156), channel_id=1, replica_groups=mesh['row'=16,'col'=16] {'col'}, dimensions={0}, use_global_device_ids=true | all-gather | bytes 557056 | tf_op jit(solution)/shard_map/all_gather | solution.py:28
  528.4 7.1 fusion.17
  535.6 28.7 %scatter_fusion.3 = f32[64,128,32]{1,2,0:T(8,128)S(1)} fusion(f32[64,128,32]{1,2,0:T(8,128)S(1)} %broadcast.195.clone.2, s32[320]{0:T(512)S(1)} %fusion.47, f32[320,128,32]{1,2,0:T(8,128)} %fusion.17), kind=kCustom, calls=%fused_computation.7 | custom fusion | flops 1310720 | bytes 15729920 | tf_op jit(solution)/shard_map/scatter-add | solution.py:39
  564.3 2.6 copy.60
  567.0 4.1 reshape.161
  571.1 2.6 reduce-scatter.9.cloned.1.call-done
  574.8 72.7 %reduce-scatter.11.cloned.1.call-done = f32[128,128]{1,0:T(8,128)} async-done(((f32[2048,128]{1,0:T(8,128)}), f32[128,128]{1,0:T(8,128)}) %reduce-scatter.11.cloned.1.call-update) | async-done | bytes 65552 | tf_op jit(solution)/shard_map/reduce_scatter | solution.py:40
  648.8 72.7 %psum.30 = f32[128,64]{1,0:T(8,128)S(1)} all-reduce(f32[128,64]{1,0:T(8,128)S(1)} %fusion.28), channel_id=1, replica_groups=mesh['row'=16,'col'=16] {'row','col'}, use_global_device_ids=true, to_apply=%region_15.18 | all-reduce | flops 8192 | bytes 65536 | tf_op jit(solution)/shard_map/psum | solution.py:53
  721.9 11.7 %cholesky.88 = f32[128,128]{1,0:T(8,128)S(1)} custom-call(f32[128,128]{1,0:T(8,128)S(1)} %fusion.34), custom_call_target="Cholesky" | custom-call | tf_op jit(solution)/shard_map/jit(cholesky)/cholesky | solution.py:8
  734.9 9.8 %custom-call.22 = f32[1,128,128]{1,2,0:T(8,128)S(1)} custom-call(f32[1,128,128]{2,1,0:T(8,128)S(1)} %fusion.25), custom_call_target="InvertDiagBlocksLowerTriangular" | custom-call | tf_op jit(solution)/shard_map/triangular_solve | solution.py:10
  745.7 73.5 %psum.31 = f32[32,32]{0,1:T(8,128)S(1)} all-reduce(f32[32,32]{0,1:T(8,128)S(1)} %fusion.52), channel_id=1, replica_groups=mesh['row'=16,'col'=16] {'row','col'}, use_global_device_ids=true, to_apply=%region_18.21 | all-reduce | flops 1024 | bytes 8192 | tf_op jit(solution)/shard_map/psum | solution.py:62
  819.2 2.9 cholesky.125
  (100 shorter events, 42.6 us)
Async XLA Ops:
  7.2 42.8 %copy-start.3 = (s32[1,1,320]{2,1,0:T(1,128)S(1)}, s32[1,1,320]{2,1,0:T(1,128)}, u32[]{:S(2)}) copy-start(s32[1,1,320]{2,1,0:T(1,128)} %param.12) | copy-start | bytes 3844
  7.2 42.9 %copy-start.4 = (s32[1,1,320]{2,1,0:T(1,128)S(1)}, s32[1,1,320]{2,1,0:T(1,128)}, u32[]{:S(2)}) copy-start(s32[1,1,320]{2,1,0:T(1,128)} %param.11) | copy-start | bytes 3844
  7.2 162.2 %reduce-scatter.5.cloned.1.call-start = ((), (), s32[]{:S(2)}) async-start(), calls=%async_computation.4 | async-start | bytes 1114112 | tf_op jit(solution)/shard_map/reduce_scatter | solution.py:36
  97.7 145.5 %reduce-scatter.7.cloned.1.call-start = ((), (), s32[]{:S(2)}) async-start(), calls=%async_computation.5 | async-start | bytes 1114112 | tf_op jit(solution)/shard_map/reduce_scatter | solution.py:40
  159.6 6.9 copy-start.2
  159.6 6.9 copy-start
  166.4 407.4 %reduce-scatter.9.cloned.1.call-start = ((), (), s32[]{:S(2)}) async-start(), calls=%async_computation.6 | async-start | bytes 1114112 | tf_op jit(solution)/shard_map/reduce_scatter | solution.py:36
  416.5 328.9 %copy-start.1 = (bf16[512,32]{0,1:T(8,128)(2,1)}, bf16[512,32]{0,1:T(8,128)(2,1)S(1)}, u32[]{:S(2)}) copy-start(bf16[512,32]{0,1:T(8,128)(2,1)S(1)} %get-tuple-element.5) | copy-start | bytes 98308
  502.9 144.6 %reduce-scatter.11.cloned.1.call-start = ((), (), s32[]{:S(2)}) async-start(), calls=%async_computation.7 | async-start | bytes 1114112 | tf_op jit(solution)/shard_map/reduce_scatter | solution.py:40
Sparse Core Ops, SparseCore 0:
  97.9 71.4 reduce-scatter.4
  172.0 71.1 reduce-scatter.6
  503.1 70.6 reduce-scatter.8
  576.3 71.1 reduce-scatter.10
where the time goes:
time: 839 us; the launch traced here: 833 us
  blocking collectives  412 us (49%)
  other arithmetic  171 us (20%)
  waiting for transfers between devices  151 us (18%)
  local copies, waits for them, and re-layouts  48.9 us (6%)
  matrix products  36.6 us (4%)
  between operations  14.3 us (2%)
    psum x2, blocking collectives, extend(): squares = lax.psum(local_rem, ('row', 'col')) / nodes  147 us
    psum x2, blocking collectives, extend(): summed = lax.psum(local_part, ('row', 'col'))  146 us
    reduce_scatter x2, waiting for transfers between devices, similarity(): lax.psum_scatter(backward_cols.reshape(-1, 128), 'row', scatter_dimension...  145 us
    all_gather x2, blocking collectives, similarity(): lax.all_gather(packed, 'row', axis=0, tiled=True)  75.9 us
    scatter-add x2, other arithmetic, similarity(): jnp.zeros(column_block.shape, jnp.float32).at[cols_index]  57.4 us
    scatter-add x2, other arithmetic, similarity(): jnp.zeros(row_block.shape, jnp.float32).at[rows_index].add(forward_terms)  57.4 us
    all_gather x2, blocking collectives, similarity(): lax.all_gather(packed, 'col', axis=0, tiled=True)  43.1 us
    another operation x6, other arithmetic, solve_gram(): factor = jnp.linalg.cholesky(gram_matrix)  21.8 us
  transfers between devices with their start and end apart: 4, of which 4 were waited for; matrix products, arithmetic and copies ran while one was open for 11% of the time, Pallas kernels for 0%

commit v1 on v0

v1 whole, which is shorter than its diff:
```python
import jax
import jax.numpy as jnp
from jax import lax
from jax.experimental import pallas as pl
from jax.experimental.pallas import tpu as pltpu
from jax.sharding import PartitionSpec as P

F32 = jnp.float32
BF16 = jnp.bfloat16
EDGE = 128
BLK = 32
STEP_TILES = 16
NT = (((1,), (1,)), ((), ()))
NN = (((1,), (0,)), ((), ()))
TN = (((0,), (0,)), ((), ()))
VMEM = pltpu.VMEM


def dot(a, b, dims=NN):
    return lax.dot_general(a, b, dims, preferred_element_type=F32)


def dot_exact(a, b, dims=NN):
    return lax.dot_general(
        a, b, dims, preferred_element_type=F32, precision=lax.Precision.HIGHEST
    )


def iota(shape, axis):
    return lax.broadcasted_iota(jnp.int32, shape, axis)


def eye(n, dtype):
    return jnp.where(iota((n, n), 0) == iota((n, n), 1), 1.0, 0.0).astype(dtype)


def whole(count):
    return [pl.BlockSpec(memory_space=VMEM)] * count


def call(body, out_shape, args, scratch=(), vmem=24 << 20):
    return pl.pallas_call(
        body,
        out_shape=out_shape,
        in_specs=whole(len(args)),
        out_specs=jax.tree.map(lambda _: pl.BlockSpec(memory_space=VMEM), out_shape),
        scratch_shapes=list(scratch),
        compiler_params=pltpu.CompilerParams(vmem_limit_bytes=vmem),
    )(*args)


def shape(dims, dtype):
    return jax.ShapeDtypeStruct(dims, dtype)


def spread(block, scale, send_ref, own_ref):
    for j in range(block.shape[1] // EDGE):
        lanes = slice(j * EDGE, (j + 1) * EDGE)
        piece = (scale[:, lanes] * block[:, lanes].astype(F32)).astype(BF16)
        own_ref[j] = piece
        for k in range(send_ref.shape[0]):
            send_ref[k, j] = piece


def prep_body(start_ref, stored_ref, level_ref, levels_ref, send_ref, own_ref, scale_ref, basis_ref):
    table = jnp.broadcast_to(levels_ref[...], (EDGE, EDGE)).T
    for j in range(level_ref.shape[1] // EDGE):
        lanes = slice(j * EDGE, (j + 1) * EDGE)
        member = level_ref[:, lanes] == iota((EDGE, EDGE), 0)
        scale_ref[:, lanes] = jnp.sum(jnp.where(member, table, 0.0), axis=0, keepdims=True)
    start = dot(eye(BLK, BF16), start_ref[...], NT).astype(BF16)
    stored = dot(eye(2 * BLK, BF16), stored_ref[...], NT).astype(BF16)
    basis_ref[0 : 2 * BLK] = stored
    basis_ref[2 * BLK :] = start
    spread(start, scale_ref[...], send_ref, own_ref)


def tile_body(rows_ref, cols_ref, tiles_ref, col_blk, row_blk, fwd_ref, bwd_ref, fwd_acc, bwd_acc):
    step = pl.program_id(0)

    @pl.when(step == 0)
    def _():
        fwd_acc[...] = jnp.zeros_like(fwd_acc)
        bwd_acc[...] = jnp.zeros_like(bwd_acc)

    for t in range(STEP_TILES):
        r = rows_ref[step * STEP_TILES + t]
        c = cols_ref[step * STEP_TILES + t]
        tile = tiles_ref[t]
        fwd_acc[r] += dot(col_blk[c], tile, NT)
        bwd_acc[c] += dot(row_blk[r], tile)

    @pl.when(step == pl.num_programs(0) - 1)
    def _():
        fwd_ref[...] = fwd_acc[...].astype(BF16)
        bwd_ref[...] = bwd_acc[...].astype(BF16)


def tile_pass(rows, cols, tiles, col_blk, row_blk):
    count = tiles.shape[0]
    acc = (row_blk.shape[0], BLK, EDGE)
    blk = pl.BlockSpec(acc, lambda i, *_: (0, 0, 0))
    return pl.pallas_call(
        tile_body,
        out_shape=(shape(acc, BF16), shape(acc, BF16)),
        grid_spec=pltpu.PrefetchScalarGridSpec(
            num_scalar_prefetch=2,
            grid=(count // STEP_TILES,),
            in_specs=[
                pl.BlockSpec((STEP_TILES, EDGE, EDGE), lambda i, *_: (i, 0, 0)),
                blk,
                blk,
            ],
            out_specs=(blk, blk),
            scratch_shapes=[pltpu.VMEM(acc, F32), pltpu.VMEM(acc, F32)],
        ),
        compiler_params=pltpu.CompilerParams(vmem_limit_bytes=24 << 20),
    )(rows, cols, tiles, col_blk, row_blk)


def image_of(fwd_ref, bwd_ref, own_ref, scale_ref):
    pieces = []
    for j in range(own_ref.shape[0]):
        total = own_ref[j].astype(F32)
        for k in range(fwd_ref.shape[0]):
            total += fwd_ref[k, j].astype(F32) + bwd_ref[k, j].astype(F32)
        pieces.append((scale_ref[:, j * EDGE : (j + 1) * EDGE] * total).astype(BF16))
    return jnp.concatenate(pieces, axis=1)


def first_image_body(fwd_ref, bwd_ref, own_ref, scale_ref, basis_ref, all_ref, pay_ref):
    image = image_of(fwd_ref, bwd_ref, own_ref, scale_ref)
    basis = basis_ref[...]
    every = jnp.concatenate([image, basis], axis=0)
    all_ref[...] = every
    stored = basis[0 : 2 * BLK]
    mine = dot(stored, stored, NT)
    pay = jnp.concatenate(
        [
            dot(image, every, NT),
            dot(basis[2 * BLK :], every, NT),
            jnp.concatenate([mine[:BLK], mine[BLK:]], axis=1),
        ],
        axis=0,
    )
    for k in range(pay_ref.shape[0]):
        pay_ref[k] = pay


def second_image_body(fwd_ref, bwd_ref, own_ref, scale_ref, basis_ref, image_ref, pay_ref):
    image = image_of(fwd_ref, bwd_ref, own_ref, scale_ref)
    image_ref[...] = image
    basis = basis_ref[...]
    square = dot(image, image, NT)
    pay = jnp.concatenate(
        [
            dot(image, basis, NT),
            dot(basis[:BLK], basis, NT),
            jnp.concatenate([square, jnp.zeros((BLK, EDGE - BLK), F32)], axis=1),
        ],
        axis=0,
    )
    for k in range(pay_ref.shape[0]):
        pay_ref[k] = pay


def middle_body(got_ref, pay_ref):
    total = jnp.sum(got_ref[...], axis=0)
    for k in range(pay_ref.shape[0]):
        pay_ref[k] = total


def reduce_all(pay):
    got = lax.all_to_all(pay, "row", 0, 0)
    again = call(middle_body, shape(got.shape, F32), (got,))
    return lax.all_to_all(again, "col", 0, 0)


def eliminate(ref, count, first_lane, above):
    rows, width = ref.shape

    def body(k, carry):
        matrix = ref[...]
        row = ref[pl.ds(k, 1), :]
        here = iota((rows, EDGE), 1) == first_lane + k
        column = jnp.sum(jnp.where(here, matrix[:, :EDGE], 0.0), axis=1, keepdims=True)
        pivot = jnp.sum(jnp.where(here[:1], row[:, :EDGE], 0.0), axis=1, keepdims=True)
        index = iota((rows, 1), 0)
        if above:
            scaled = row / pivot
            ref[...] = jnp.where(index == k, scaled, matrix - column * scaled)
        else:
            scaled = row / jnp.sqrt(pivot)
            later = jnp.where(index > k, column / jnp.sqrt(pivot), 0.0)
            ref[...] = jnp.where(index == k, scaled, matrix - later * scaled)
        return carry

    lax.fori_loop(0, count, body, 0)


def pad_lanes(a, width=EDGE):
    return jnp.concatenate([a, jnp.zeros((a.shape[0], width - a.shape[1]), F32)], axis=1)


def inverse_factor(small, square):
    small[...] = pad_lanes(jnp.concatenate([square, eye(BLK, F32)], axis=1))
    eliminate(small, BLK, 0, False)
    return small[:, BLK : 2 * BLK]


def emit(new, out_ref):
    out_ref[...] = dot(new, eye(BLK, BF16), TN).astype(BF16)


def first_solve_body(
    nodes, got_ref, all_ref, scale_ref, first_ref, send_ref, own_ref, next_ref, gram_ref, inv_ref, work, small
):
    got = jnp.sum(got_ref[...], axis=0)
    mine = got[2 * BLK :]
    low = jnp.concatenate(
        [got[:BLK], pltpu.roll(mine, BLK, 1), pltpu.roll(mine, EDGE - BLK, 1), got[BLK : 2 * BLK]], axis=0
    )
    row, lane = iota((EDGE, EDGE), 0), iota((EDGE, EDGE), 1)
    inner_row = (row >= BLK) & (row < 3 * BLK)
    inner_lane = (lane >= BLK) & (lane < 3 * BLK)
    gram = jnp.where(inner_row & jnp.logical_not(inner_lane), low.T, low)
    gram_ref[...] = gram
    work[:, :EDGE] = gram[BLK:]
    work[:, EDGE:] = jnp.where(iota((3 * BLK, EDGE), 0) + BLK == iota((3 * BLK, EDGE), 1), 1.0, 0.0)
    eliminate(work, 3 * BLK, BLK, True)
    inv_ref[...] = jnp.concatenate([jnp.zeros((BLK, EDGE), F32), work[:, EDGE:]], axis=0)
    tall = jnp.concatenate(
        [jnp.where(row[:BLK] == lane[:BLK], 1.0, 0.0), -work[:, :EDGE]], axis=0
    )
    mix = tall.T[:BLK].astype(BF16)
    wide = mix.astype(F32)
    squares = dot_exact(dot_exact(wide, gram), wide, NT) / nodes
    factor = inverse_factor(small, squares)
    remainder = dot(mix, all_ref[...])
    new = dot_exact(factor, remainder).astype(BF16)
    emit(new, first_ref)
    next_ref[...] = jnp.concatenate([new, all_ref[BLK:]], axis=0)
    spread(new, scale_ref[...], send_ref, own_ref)


def second_solve_body(nodes, got_ref, image_ref, basis_ref, gram_ref, inv_ref, second_ref, small):
    got = jnp.sum(got_ref[...], axis=0)
    cross, fresh, square = got[:BLK], got[BLK : 2 * BLK], got[2 * BLK :, :BLK]
    row, lane = iota((EDGE, EDGE), 0), iota((EDGE, EDGE), 1)
    inv = inv_ref[...]
    reach = dot_exact(fresh, inv)
    schur = fresh[:, :BLK] - dot_exact(reach, fresh, NT)
    small[...] = pad_lanes(jnp.concatenate([schur, eye(BLK, F32)], axis=1))
    eliminate(small, BLK, 0, True)
    newest = dot_exact(cross[:, :BLK] - dot_exact(cross, reach, NT), small[:, BLK : 2 * BLK])
    older = dot_exact(cross, inv) - dot_exact(newest, reach)
    coef = jnp.where(lane[:BLK] < BLK, pad_lanes(newest), older).astype(BF16)
    wide = coef.astype(F32)
    full = jnp.concatenate([fresh, jnp.zeros((3 * BLK, EDGE), F32)], axis=0)
    gram = jnp.where(row < BLK, full, jnp.where(lane < BLK, full.T, gram_ref[...]))
    mixed = dot_exact(wide, cross, NT)
    squares = (square - mixed - mixed.T + dot_exact(dot_exact(wide, gram), wide, NT)) / nodes
    factor = inverse_factor(small, squares)
    remainder = image_ref[...].astype(F32) - dot(coef, basis_ref[...])
    emit(dot_exact(factor, remainder).astype(BF16), second_ref)


def per_device(tiles, tile_rows, tile_cols, node_level, level_scale, stored_basis, start_block):
    tile_stack = tiles.reshape(tiles.shape[2:])
    rows, cols = tile_rows.reshape(-1), tile_cols.reshape(-1)
    side = lax.axis_size("row")
    held = stored_basis.shape[0]
    nodes = held * side * lax.axis_size("col")
    pieces = held // EDGE
    send_shape = shape((side, pieces, BLK, EDGE), BF16)
    own_shape = shape((pieces, BLK, EDGE), BF16)

    def product(send):
        col_blk = lax.all_to_all(send, "row", 0, 0).reshape(-1, BLK, EDGE)
        row_blk = lax.all_to_all(send, "col", 0, 0).reshape(-1, BLK, EDGE)
        fwd, bwd = tile_pass(rows, cols, tile_stack, col_blk, row_blk)
        fwd = lax.all_to_all(fwd.reshape(send.shape), "col", 0, 0)
        bwd = lax.all_to_all(bwd.reshape(send.shape), "row", 0, 0)
        return fwd, bwd

    send, own, scale, basis = call(
        prep_body,
        (send_shape, own_shape, shape((1, held), F32), shape((3 * BLK, held), BF16)),
        (start_block, stored_basis, node_level.reshape(1, -1), level_scale.reshape(1, -1)),
    )
    fwd, bwd = product(send)
    pay_shape = shape((side, 3 * BLK, EDGE), F32)
    every, pay = call(
        first_image_body, (shape((EDGE, held), BF16), pay_shape), (fwd, bwd, own, scale, basis)
    )
    got = reduce_all(pay)
    square_shape = shape((EDGE, EDGE), F32)
    first, send, own, basis, gram, inv = call(
        lambda *refs: first_solve_body(nodes, *refs),
        (
            shape((held, BLK), BF16),
            send_shape,
            own_shape,
            shape((EDGE, held), BF16),
            square_shape,
            square_shape,
        ),
        (got, every, scale),
        (pltpu.VMEM((3 * BLK, 2 * EDGE), F32), pltpu.VMEM((BLK, EDGE), F32)),
    )
    fwd, bwd = product(send)
    image, pay = call(
        second_image_body, (shape((BLK, held), BF16), pay_shape), (fwd, bwd, own, scale, basis)
    )
    got = reduce_all(pay)
    second = call(
        lambda *refs: second_solve_body(nodes, *refs),
        shape((held, BLK), BF16),
        (got, image, basis, gram, inv),
        (pltpu.VMEM((BLK, EDGE), F32),),
    )
    return (first, second)


def solution(mesh):
    return jax.shard_map(
        per_device,
        mesh=mesh,
        in_specs=(
            P("row", "col", None, None, None),
            P("row", "col", None),
            P("row", "col", None),
            P(("row", "col")),
            P(),
            P(("row", "col"), None),
            P(("row", "col"), None),
        ),
        out_specs=(P(("row", "col"), None), P(("row", "col"), None)),
        check_vma=False,
    )
```

time: 839 us -> 300 us (0.36)
  blocking collectives: 412 us -> 194 us
  other arithmetic: 171 us -> 1.4 us
  waiting for transfers between devices: 151 us -> 28.3 us
  Pallas kernels: 0 us -> 49 us
  local copies, waits for them, and re-layouts: 48.9 us -> 8.58 us
  matrix products: 36.6 us -> 0 us
  starting transfers between devices: 0.16 us -> 14.4 us
  between operations: 14.3 us -> 0.74 us
    psum x4 -> x0, blocking collectives: 293 us -> none  [the longest x2 147 us: extend(): squares = lax.psum(local_rem, ('row', 'col')) / nodes]
    all_to_all x0 -> x10, blocking collectives: none -> 194 us  [the longest x2 51.4 us: reduce_all(): got = lax.all_to_all(pay, 'row', 0, 0)]
    reduce_scatter x4 -> x0, waiting for transfers between devices: 151 us -> none  [the longest x2 145 us: similarity(): lax.psum_scatter(backward_cols.reshape(-1, 128), 'row', scatter_dimension...]
    all_gather x4 -> x0, blocking collectives: 119 us -> none  [the longest x2 75.9 us: similarity(): lax.all_gather(packed, 'row', axis=0, tiled=True)]
    scatter-add x4 -> x0, other arithmetic: 115 us -> none  [the longest x2 57.4 us: similarity(): jnp.zeros(column_block.shape, jnp.float32).at[cols_index]]
    another operation x20 -> x0, other arithmetic: 53.7 us -> none  [the longest x6 21.8 us: solve_gram(): factor = jnp.linalg.cholesky(gram_matrix)]
    pallas_call x0 -> x9, Pallas kernels: none -> 49 us  [the longest x7 25.3 us: call(): pl.pallas_call(body, out_shape=out_shape, in_specs=whole(len(args)), out_...]
    dot_general x10 -> x0, matrix products: 34.6 us -> none  [the longest x2 19.4 us: similarity(): jnp.einsum('tij,tjk->tik', tile_stack, column_block[cols_index], preferre...]
  transfers between devices with their start and end apart: 4 -> 2, of which waited for: 4 -> 2; matrix products, arithmetic and copies ran while one was open for 11% -> 1% of each run, Pallas kernels for 0% -> 0%
where the time goes in v1:
time: 300 us; the launch traced here: 296 us
  blocking collectives  194 us (65%)
  Pallas kernels  49 us (16%)
  waiting for transfers between devices  28.3 us (9%)
  starting transfers between devices  14.4 us (5%)
  local copies, waits for them, and re-layouts  8.58 us (3%)
    all_to_all x2, blocking collectives, reduce_all(): got = lax.all_to_all(pay, 'row', 0, 0)  51.4 us
    all_to_all x2, blocking collectives, product(): bwd = lax.all_to_all(bwd.reshape(send.shape), 'row', 0, 0)  42.2 us
    all_to_all x2, blocking collectives, product(): row_blk = lax.all_to_all(send, 'col', 0, 0).reshape(-1, BLK, EDGE)  32.1 us
    all_to_all x2, blocking collectives, product(): fwd = lax.all_to_all(fwd.reshape(send.shape), 'col', 0, 0)  29.6 us
    pallas_call x7, Pallas kernels, call(): pl.pallas_call(body, out_shape=out_shape, in_specs=whole(len(args)), out_...  25.3 us
    pallas_call x2, Pallas kernels, tile_pass(): pl.pallas_call(tile_body, out_shape=(shape(acc, BF16), shape(acc, BF16)),...  23.7 us
    all_to_all x1, blocking collectives, product(): col_blk = lax.all_to_all(send, 'row', 0, 0).reshape(-1, BLK, EDGE)  21.1 us
    all_to_all x1, blocking collectives, reduce_all(): return lax.all_to_all(again, 'col', 0, 0)  17.5 us
  transfers between devices with their start and end apart: 2, of which 2 were waited for; matrix products, arithmetic and copies ran while one was open for 1% of the time, Pallas kernels for 0%

profile of v1, /device:TPU:4, one launch (start us, length us, event | category | flops | bytes accessed | tf_op | source)
XLA Modules:
  0.0 296.4 jit_solution(8412094226694970552)
XLA Ops:
  0.6 1.0 copy.10.stored_ref
  1.6 0.9 copy.9.start_ref
  2.5 0.7 copy-done.1
  3.2 0.7 copy-done.2
  3.8 1.0 shard_map.86
  4.8 17.2 %all_to_all.60 = bf16[16,4,32,128]{3,2,1,0:T(8,128)(2,1)S(1)} all-to-all(bf16[16,4,32,128]{3,2,1,0:T(8,128)(2,1)} %get-tuple-element.20), channel_id=1, replica_groups=mesh['row'=16,'col'=16] {'col'}, dimensions={0} | all-to-all | bytes 1048576 | tf_op jit(solution)/shard_map/all_to_all | solution.py:280
  22.0 9.2 %all-to-all-start = ((bf16[16,4,32,128]{3,2,1,0:T(8,128)(2,1)}), bf16[16,4,32,128]{3,2,1,0:T(8,128)(2,1)S(1)}, u32[]{:S(2)}, u32[]{:S(2)}) async-start(bf16[16,4,32,128]{3,2,1,0:T(8,128)(2,1)} %get-tuple-element.20), calls=%async_computation | async-start | bytes 1048576 | tf_op jit(solution)/shard_map/all_to_all | solution.py:279
  31.2 0.7 reduce.rows_ref
  31.9 0.7 reduce.1.cols_ref
  32.6 16.5 %all-to-all-done = bf16[16,4,32,128]{3,2,1,0:T(8,128)(2,1)S(1)} async-done(((bf16[16,4,32,128]{3,2,1,0:T(8,128)(2,1)}), bf16[16,4,32,128]{3,2,1,0:T(8,128)(2,1)S(1)}, u32[]{:S(2)}, u32[]{:S(2)}) %all-to-all-start) | async-done | bytes 524320 | tf_op jit(solution)/shard_map/all_to_all | solution.py:279
  49.1 4.0 %copy-done = bf16[1,1,320,128,128]{4,3,2,1,0:T(8,128)(2,1)S(1)} copy-done((bf16[1,1,320,128,128]{4,3,2,1,0:T(8,128)(2,1)S(1)}, bf16[1,1,320,128,128]{4,3,2,1,0:T(8,128)(2,1)}, u32[]{:S(2)}) %copy-start) | copy-done | bytes 10485784
  53.1 11.8 %shard_map.87 = (bf16[64,32,128]{2,1,0:T(8,128)(2,1)S(1)}, bf16[64,32,128]{2,1,0:T(8,128)(2,1)S(1)}) custom-call(s32[320]{0:T(512)S(1)} %reduce.rows_ref, s32[320]{0:T(512)S(1)} %reduce.1.cols_ref, bf16[320,128,128]{2,1,0:T(8,128)(2,1)S(1)} %bitcast.11, bf16[64,32,128]{2,1,0:T(8,128)(2,1)S(1)} %bitcast.16, bf16[64,32,128]{2,1,0:T(8,128)(2,1)S(1)} %bitcast.15), custom_call_target="tpu_custom_call" | custom-call | tf_op jit(solution)/shard_map/pallas_call | solution.py:103
  64.9 14.9 %all_to_all.61.fwd_ref = bf16[16,4,32,128]{3,2,1,0:T(8,128)(2,1)S(1)} all-to-all(bf16[16,4,32,128]{3,2,1,0:T(8,128)(2,1)S(1)} %bitcast.22), channel_id=1, replica_groups=mesh['row'=16,'col'=16] {'col'}, dimensions={0} | all-to-all | bytes 1048576 | tf_op jit(solution)/shard_map/all_to_all | solution.py:282
  79.8 21.1 %all_to_all.62.bwd_ref = bf16[16,4,32,128]{3,2,1,0:T(8,128)(2,1)S(1)} all-to-all(bf16[16,4,32,128]{3,2,1,0:T(8,128)(2,1)S(1)} %bitcast.21), channel_id=1, replica_groups=mesh['row'=16,'col'=16] {'row'}, dimensions={0} | all-to-all | bytes 1048576 | tf_op jit(solution)/shard_map/all_to_all | solution.py:283
  100.9 0.4 shard_map.88
  101.3 25.8 %all_to_all.63.got_ref = f32[16,96,128]{2,1,0:T(8,128)S(1)} all-to-all(f32[16,96,128]{2,1,0:T(8,128)S(1)} %get-tuple-element.26), channel_id=1, replica_groups=mesh['row'=16,'col'=16] {'row'}, dimensions={0} | all-to-all | bytes 1572864 | tf_op jit(solution)/shard_map/all_to_all | solution.py:174
  127.0 0.1 shard_map.89
  127.1 17.5 %all_to_all.64.refs_0_ = f32[16,96,128]{2,1,0:T(8,128)S(1)} all-to-all(f32[16,96,128]{2,1,0:T(8,128)S(1)} %shard_map.89), channel_id=1, replica_groups=mesh['row'=16,'col'=16] {'col'}, dimensions={0} | all-to-all | bytes 1572864 | tf_op jit(solution)/shard_map/all_to_all | solution.py:176
  144.7 14.3 %shard_map.90 = (bf16[512,32]{1,0:T(8,128)(2,1)S(1)}, bf16[16,4,32,128]{3,2,1,0:T(8,128)(2,1)S(1)}, bf16[4,32,128]{2,1,0:T(8,128)(2,1)S(1)}, bf16[128,512]{1,0:T...) custom-call(f32[16,96,128]{2,1,0:T(8,128)S(1)} %all_to_all.64.refs_0_, ...), custom_call_target="tpu_custom_call" | custom-call | tf_op jit(solution)/shard_map/pallas_call | solution.py:42
  159.0 14.9 %all_to_all.65 = bf16[16,4,32,128]{3,2,1,0:T(8,128)(2,1)S(1)} all-to-all(bf16[16,4,32,128]{3,2,1,0:T(8,128)(2,1)S(1)} %get-tuple-element.29), channel_id=1, replica_groups=mesh['row'=16,'col'=16] {'col'}, dimensions={0} | all-to-all | bytes 1048576 | tf_op jit(solution)/shard_map/all_to_all | solution.py:280
  173.9 21.1 %all_to_all.66 = bf16[16,4,32,128]{3,2,1,0:T(8,128)(2,1)S(1)} all-to-all(bf16[16,4,32,128]{3,2,1,0:T(8,128)(2,1)S(1)} %get-tuple-element.29), channel_id=1, replica_groups=mesh['row'=16,'col'=16] {'row'}, dimensions={0} | all-to-all | bytes 1048576 | tf_op jit(solution)/shard_map/all_to_all | solution.py:279
  195.1 11.8 %shard_map.91 = (bf16[64,32,128]{2,1,0:T(8,128)(2,1)S(1)}, bf16[64,32,128]{2,1,0:T(8,128)(2,1)S(1)}) custom-call(s32[320]{0:T(512)S(1)} %reduce.rows_ref, s32[320]{0:T(512)S(1)} %reduce.1.cols_ref, bf16[320,128,128]{2,1,0:T(8,128)(2,1)S(1)} %bitcast.14, bf16[64,32,128]{2,1,0:T(8,128)(2,1)S(1)} %bitcast.18, bf16[64,32,128]{2,1,0:T(8,128)(2,1)S(1)} %bitcast.17), custom_call_target="tpu_custom_call" | custom-call | tf_op jit(solution)/shard_map/pallas_call | solution.py:103
  206.9 14.8 %all_to_all.67.fwd_ref = bf16[16,4,32,128]{3,2,1,0:T(8,128)(2,1)S(1)} all-to-all(bf16[16,4,32,128]{3,2,1,0:T(8,128)(2,1)S(1)} %bitcast.20), channel_id=1, replica_groups=mesh['row'=16,'col'=16] {'col'}, dimensions={0} | all-to-all | bytes 1048576 | tf_op jit(solution)/shard_map/all_to_all | solution.py:282
  221.6 21.1 %all_to_all.68.bwd_ref = bf16[16,4,32,128]{3,2,1,0:T(8,128)(2,1)S(1)} all-to-all(bf16[16,4,32,128]{3,2,1,0:T(8,128)(2,1)S(1)} %bitcast.19), channel_id=1, replica_groups=mesh['row'=16,'col'=16] {'row'}, dimensions={0} | all-to-all | bytes 1048576 | tf_op jit(solution)/shard_map/all_to_all | solution.py:283
  242.7 0.4 shard_map.92
  243.1 25.7 %all_to_all.69.got_ref = f32[16,96,128]{2,1,0:T(8,128)S(1)} all-to-all(f32[16,96,128]{2,1,0:T(8,128)S(1)} %get-tuple-element.34), channel_id=1, replica_groups=mesh['row'=16,'col'=16] {'row'}, dimensions={0} | all-to-all | bytes 1572864 | tf_op jit(solution)/shard_map/all_to_all | solution.py:174
  268.8 1.0 shard_map.93
  269.7 5.2 %all-to-all-start.11 = ((f32[16,96,128]{2,1,0:T(8,128)}), f32[16,96,128]{2,1,0:T(8,128)S(1)}, u32[]{:S(2)}, u32[]{:S(2)}) async-start(f32[16,96,128]{2,1,0:T(8,128)} %shard_map.93), calls=%async_computation.11 | async-start | bytes 1572864 | tf_op jit(solution)/shard_map/all_to_all | solution.py:176
  274.9 0.7 copy.11
  275.6 11.8 %all-to-all-done.11.refs_0_ = f32[16,96,128]{2,1,0:T(8,128)S(1)} async-done(((f32[16,96,128]{2,1,0:T(8,128)}), f32[16,96,128]{2,1,0:T(8,128)S(1)}, u32[]{:S(2)}, u32[]{:S(2)}) %all-to-all-start.11) | async-done | bytes 786464 | tf_op jit(solution)/shard_map/all_to_all | solution.py:176
  287.5 8.2 %shard_map.94 = bf16[512,32]{1,0:T(8,128)(2,1)S(1)} custom-call(f32[16,96,128]{2,1,0:T(8,128)S(1)} %all-to-all-done.11.refs_0_, bf16[32,512]{1,0:T(8,128)(2,1)S(1)} %get-tuple-element.35.refs_1_, bf16[128,512]{1,0:T(8,128)(2,1)S(1)} %get-tuple-element.33.basis_ref.refs_2_, f32[128,128]{1,0:T(8,128)S(1)} %get-tuple-element.36.refs_3_, ...), custom_call_target="tpu_custom_call" | custom-call | tf_op jit(solution)/shard_map/pallas_call | solution.py:42
  295.7 0.7 copy.12
  (10 shorter events, 0.0 us)
Async XLA Ops:
  2.5 0.7 copy-start.1
  3.2 0.7 copy-start.2
  22.0 27.1 %all-to-all-start = ((bf16[16,4,32,128]{3,2,1,0:T(8,128)(2,1)}), bf16[16,4,32,128]{3,2,1,0:T(8,128)(2,1)S(1)}, u32[]{:S(2)}, u32[]{:S(2)}) async-start(bf16[16,4,32,128]{3,2,1,0:T(8,128)(2,1)} %get-tuple-element.20), calls=%async_computation | async-start | bytes 1048576 | tf_op jit(solution)/shard_map/all_to_all | solution.py:279
  49.1 4.0 %copy-start = (bf16[1,1,320,128,128]{4,3,2,1,0:T(8,128)(2,1)S(1)}, bf16[1,1,320,128,128]{4,3,2,1,0:T(8,128)(2,1)}, u32[]{:S(2)}) copy-start(bf16[1,1,320,128,128]{4,3,2,1,0:T(8,128)(2,1)} %param.7) | copy-start | bytes 31457284
  53.1 141.9 %slice-start = ((s8[10485760]{0:T(1024)(128)(4,1)}), s8[4194304]{0:T(1024)(128)(4,1)S(1)}, s32[]{:S(2)}) async-start(s8[10485760]{0:T(1024)(128)(4,1)} %bitcast.12), calls=%async_computation.12 | async-start | bytes 8388608
  53.1 141.9 %slice-start.1 = ((s8[10485760]{0:T(1024)(128)(4,1)}), s8[4194304]{0:T(1024)(128)(4,1)S(1)}, s32[]{:S(2)}) async-start(s8[10485760]{0:T(1024)(128)(4,1)} %bitcast.12), calls=%async_computation.13 | async-start | bytes 8388608
  101.3 93.8 %slice-start.2 = ((s8[10485760]{0:T(1024)(128)(4,1)}), s8[2097152]{0:T(1024)(128)(4,1)S(1)}, s32[]{:S(2)}) async-start(s8[10485760]{0:T(1024)(128)(4,1)} %bitcast.12), calls=%async_computation.14 | async-start | bytes 4194304
  269.7 17.7 %all-to-all-start.11 = ((f32[16,96,128]{2,1,0:T(8,128)}), f32[16,96,128]{2,1,0:T(8,128)S(1)}, u32[]{:S(2)}, u32[]{:S(2)}) async-start(f32[16,96,128]{2,1,0:T(8,128)} %shard_map.93), calls=%async_computation.11 | async-start | bytes 1572864 | tf_op jit(solution)/shard_map/all_to_all | solution.py:176

commit v2 on v1

v2 whole, which is shorter than its diff:
```python
import jax
import jax.numpy as jnp
from jax import lax
from jax.experimental import pallas as pl
from jax.experimental.pallas import tpu as pltpu
from jax.sharding import PartitionSpec as P

F32 = jnp.float32
BF16 = jnp.bfloat16
EDGE = 128
BLK = 32
CHUNK = 80
NT = (((1,), (1,)), ((), ()))
NN = (((1,), (0,)), ((), ()))
VMEM = pltpu.VMEM


def dot(a, b, dims=NN):
    return lax.dot_general(a, b, dims, preferred_element_type=F32)


def dot_exact(a, b, dims=NN):
    return lax.dot_general(
        a, b, dims, preferred_element_type=F32, precision=lax.Precision.HIGHEST
    )


def iota(shape, axis):
    return lax.broadcasted_iota(jnp.int32, shape, axis)


def eye(n, dtype):
    return jnp.where(iota((n, n), 0) == iota((n, n), 1), 1.0, 0.0).astype(dtype)


def whole(count):
    return [pl.BlockSpec(memory_space=VMEM)] * count


def call(body, out_shape, args, scratch=(), vmem=24 << 20):
    return pl.pallas_call(
        body,
        out_shape=out_shape,
        in_specs=whole(len(args)),
        out_specs=jax.tree.map(lambda _: pl.BlockSpec(memory_space=VMEM), out_shape),
        scratch_shapes=list(scratch),
        compiler_params=pltpu.CompilerParams(vmem_limit_bytes=vmem),
    )(*args)


def shape(dims, dtype):
    return jax.ShapeDtypeStruct(dims, dtype)


def spread(block, scale, send_ref, own_ref):
    for j in range(block.shape[1] // EDGE):
        lanes = slice(j * EDGE, (j + 1) * EDGE)
        piece = (scale[:, lanes] * block[:, lanes].astype(F32)).astype(BF16)
        own_ref[j] = piece
        for k in range(send_ref.shape[0]):
            send_ref[k, j] = piece


def prep_body(start_in, stored_in, level_in, levels_in, send_ref, own_ref, scale_ref, basis_ref, level_ref, levels_ref, done):
    copies = [
        pltpu.make_async_copy(src, dst, done.at[i])
        for i, (src, dst) in enumerate(
            (
                (level_in, level_ref),
                (levels_in, levels_ref),
                (start_in, basis_ref.at[2 * BLK : 3 * BLK]),
                (stored_in, basis_ref.at[0 : 2 * BLK]),
            )
        )
    ]
    for copy in copies:
        copy.start()
    for copy in copies:
        copy.wait()
    table = jnp.broadcast_to(levels_ref[...], (EDGE, EDGE)).T
    for j in range(level_ref.shape[1] // EDGE):
        lanes = slice(j * EDGE, (j + 1) * EDGE)
        member = level_ref[:, lanes] == iota((EDGE, EDGE), 0)
        scale_ref[:, lanes] = jnp.sum(jnp.where(member, table, 0.0), axis=0, keepdims=True)
    spread(basis_ref[2 * BLK :], scale_ref[...], send_ref, own_ref)


def prep(send_shape, own_shape, start, stored, level, levels):
    held = start.shape[1]
    outs = (send_shape, own_shape, shape((1, held), F32), shape((3 * BLK, held), BF16))
    return pl.pallas_call(
        prep_body,
        out_shape=outs,
        in_specs=[pl.BlockSpec(memory_space=pltpu.HBM)] * 4,
        out_specs=tuple(whole(4)),
        scratch_shapes=[
            pltpu.VMEM(level.shape, jnp.int32),
            pltpu.VMEM(levels.shape, F32),
            pltpu.SemaphoreType.DMA((4,)),
        ],
        compiler_params=pltpu.CompilerParams(vmem_limit_bytes=58 << 20),
    )(start, stored, level, levels)


def pair_rows(first, second):
    none = jnp.zeros_like(first)
    return jnp.concatenate(
        [jnp.concatenate([first, none], axis=1), jnp.concatenate([none, second], axis=1)], axis=0
    )


def tile_body(
    pieces, me_ref, rows_ref, cols_ref, tiles_ref, col_in, near_in, far_in, bwd_out, keep_out, away_out,
    col_blk, row_blk, fwd_acc, bwd_acc, bwd_ref, keep_ref, away_ref, held, done, moved,
):
    chunks = held.shape[0]
    half = near_in.shape[0]

    def copy(i):
        part = tiles_ref.at[pl.ds(i * CHUNK, CHUNK)]
        return pltpu.make_async_copy(part, held.at[i], done.at[i])

    ins = [
        pltpu.make_async_copy(src, dst, moved.at[i])
        for i, (src, dst) in enumerate(
            ((col_in, col_blk), (near_in, row_blk.at[0:half]), (far_in, row_blk.at[half : 2 * half]))
        )
    ]
    outs = [
        pltpu.make_async_copy(src, dst, moved.at[3 + i])
        for i, (src, dst) in enumerate(((bwd_ref, bwd_out), (keep_ref, keep_out), (away_ref, away_out)))
    ]
    copy(0).start()
    for move in ins:
        move.start()
    for i in range(1, chunks):
        copy(i).start()
    fwd_acc[...] = jnp.zeros_like(fwd_acc)
    bwd_acc[...] = jnp.zeros_like(bwd_acc)
    me = me_ref[0]

    def place(row):
        apart = (row // pieces) ^ me
        return ((apart & 1) * 8 + (apart >> 1)) * pieces + (row & (pieces - 1))

    def body(i, carry):
        copy(i).wait()
        for t in range(0, CHUNK, 2):
            r = [place(rows_ref[0, 0, i * CHUNK + t + n]) for n in range(2)]
            c = [cols_ref[0, 0, i * CHUNK + t + n] for n in range(2)]
            one, two = held[i, t], held[i, t + 1]
            terms = dot(pair_rows(col_blk[c[0]], col_blk[c[1]]), jnp.concatenate([one, two], axis=1), NT)
            fwd_acc[r[0]] += terms[:BLK]
            fwd_acc[r[1]] += terms[BLK:]
            terms = dot(pair_rows(row_blk[r[0]], row_blk[r[1]]), jnp.concatenate([one, two], axis=0))
            bwd_acc[c[0]] += terms[:BLK]
            bwd_acc[c[1]] += terms[BLK:]
        return carry

    for move in ins:
        move.wait()
    lax.fori_loop(0, chunks, body, 0)
    bwd_ref[...] = bwd_acc[...].astype(BF16)
    outs[0].start()
    away_ref[...] = fwd_acc[half:].astype(BF16)
    outs[2].start()
    keep_ref[...] = fwd_acc[:half].astype(BF16)
    outs[1].start()
    for move in outs:
        move.wait()


def tile_pass(pieces, me, rows, cols, tiles, col_blk, near, far):
    count = tiles.shape[0]
    half = near.shape
    acc = col_blk.shape
    scalars = pl.BlockSpec(memory_space=pltpu.SMEM)
    return pl.pallas_call(
        lambda *refs: tile_body(pieces, *refs),
        out_shape=(shape(acc, BF16), shape(half, BF16), shape(half, BF16)),
        in_specs=[scalars] * 3 + [pl.BlockSpec(memory_space=pltpu.HBM)] + [pl.BlockSpec(memory_space=pl.ANY)] * 3,
        out_specs=tuple([pl.BlockSpec(memory_space=pl.ANY)] * 3),
        scratch_shapes=[
            pltpu.VMEM(acc, BF16),
            pltpu.VMEM(acc, BF16),
            pltpu.VMEM(acc, F32),
            pltpu.VMEM(acc, F32),
            pltpu.VMEM(acc, BF16),
            pltpu.VMEM(half, BF16),
            pltpu.VMEM(half, BF16),
            pltpu.VMEM((count // CHUNK, CHUNK, EDGE, EDGE), BF16),
            pltpu.SemaphoreType.DMA((count // CHUNK,)),
            pltpu.SemaphoreType.DMA((6,)),
        ],
        cost_estimate=pl.CostEstimate(flops=8_000_000_000, bytes_accessed=14_000_000, transcendentals=0),
        compiler_params=pltpu.CompilerParams(vmem_limit_bytes=51 << 20),
    )(me, rows, cols, tiles, col_blk, near, far)


def keep_body(in_ref, out_ref):
    pass


def arrive(a):
    return pl.pallas_call(
        keep_body,
        out_shape=shape(a.shape, a.dtype),
        in_specs=[pl.BlockSpec(memory_space=pl.ANY)],
        out_specs=pl.BlockSpec(memory_space=pl.ANY),
        input_output_aliases={0: 0},
        cost_estimate=pl.CostEstimate(flops=40_000_000_000, bytes_accessed=1_000_000, transcendentals=0),
        compiler_params=pltpu.CompilerParams(vmem_limit_bytes=1 << 20),
    )(a)


def swap(a, mask):
    return lax.ppermute(a, "col", [(i, i ^ mask) for i in range(lax.axis_size("col"))])


def gather_col(own):
    two = jnp.concatenate([own, swap(own, 2)], axis=0)
    eight = jnp.concatenate([two] + [swap(two, 4 * j) for j in range(1, 4)], axis=0)
    return (eight, swap(eight, 1))


def halve_body(parts, *refs):
    ins, outs = refs[: -1 - parts], refs[-1 - parts :]
    total = ins[0][...].astype(F32)
    for ref in ins[1:]:
        total = total + ref[...].astype(F32)
    size = total.shape[0] // (1 + parts)
    for i, ref in enumerate(outs):
        ref[...] = total[i * size : (i + 1) * size].astype(ref.dtype)


def halve(parts, keep, *arrived):
    piece = (keep.shape[0] // (1 + parts),) + keep.shape[1:]
    outs = (shape(piece, F32),) + (shape(piece, BF16),) * parts
    return call(lambda *refs: halve_body(parts, *refs), outs, (keep, *arrived))


def scatter_col(keep, send):
    keep, *sends = halve(3, keep, swap(send, 1))
    arrived = [swap(send, 4 * (j + 1)) for j, send in enumerate(sends)]
    keep, send = halve(1, keep, *arrived)
    return keep, swap(send, 2)


def image_of(keep_ref, fwd_ref, bwd_ref, own_ref, scale_ref):
    pieces = []
    for j in range(own_ref.shape[0]):
        total = own_ref[j].astype(F32) + keep_ref[j] + fwd_ref[j].astype(F32)
        for k in range(bwd_ref.shape[0]):
            total += bwd_ref[k, j].astype(F32)
        pieces.append((scale_ref[:, j * EDGE : (j + 1) * EDGE] * total).astype(BF16))
    return jnp.concatenate(pieces, axis=1)


def share(core_ref, halves, keep_ref, send_ref):
    mine = (core_ref[0] & 1) == 0
    keep_ref[...] = jnp.where(mine, halves[0], halves[1])
    send_ref[...] = jnp.where(mine, halves[1], halves[0])


def first_image_body(core_ref, keep_ref, fwd_ref, bwd_ref, own_ref, scale_ref, basis_ref, all_ref, mine_ref, send_ref):
    image = image_of(keep_ref, fwd_ref, bwd_ref, own_ref, scale_ref)
    basis = basis_ref[...]
    every = jnp.concatenate([image, basis], axis=0)
    all_ref[...] = every
    stored = basis[0 : 2 * BLK]
    inner = dot(stored, stored, NT)
    inner = jnp.concatenate([inner[:BLK], inner[BLK:]], axis=1)
    halves = [
        jnp.concatenate([dot(image, every, NT), inner[: BLK // 2]], axis=0),
        jnp.concatenate([dot(basis[2 * BLK :], every, NT), inner[BLK // 2 :]], axis=0),
    ]
    share(core_ref, halves, mine_ref, send_ref)


def second_image_body(core_ref, keep_ref, fwd_ref, bwd_ref, own_ref, scale_ref, basis_ref, image_ref, mine_ref, send_ref):
    image = image_of(keep_ref, fwd_ref, bwd_ref, own_ref, scale_ref)
    image_ref[...] = image
    basis = basis_ref[...]
    square = dot(image, image, NT)
    square = jnp.concatenate([square[8 * i : 8 * i + 8] for i in range(4)], axis=1)
    halves = [
        jnp.concatenate([dot(image, basis, NT), square], axis=0),
        jnp.concatenate([dot(basis[:BLK], basis, NT), jnp.zeros((8, EDGE), F32)], axis=0),
    ]
    share(core_ref, halves, mine_ref, send_ref)


def image_call(body, out, rows, core, args):
    half = shape((rows, EDGE), F32)
    return pl.pallas_call(
        body,
        out_shape=(out, half, half),
        in_specs=[pl.BlockSpec(memory_space=pltpu.SMEM)] + whole(len(args)),
        out_specs=tuple(whole(3)),
        compiler_params=pltpu.CompilerParams(vmem_limit_bytes=24 << 20),
    )(core, *args)


def repeat_body(*refs):
    total = refs[0][...]
    for ref in refs[1:-1]:
        total = total + ref[...]
    total = total.reshape((-1,) + refs[-1].shape[1:]).sum(axis=0)
    for k in range(refs[-1].shape[0]):
        refs[-1][k] = total


def reduce_all(keep, send):
    side = lax.axis_size("row")
    out = shape((side,) + keep.shape, F32)
    got = lax.all_to_all(call(repeat_body, out, (keep, swap(send, 1))), "row", 0, 0)
    return lax.all_to_all(call(repeat_body, out, (got,)), "col", 0, 0)


def sum_halves(got_ref):
    halves = []
    for core in range(2):
        total = got_ref[core]
        for k in range(core + 2, got_ref.shape[0], 2):
            total = total + got_ref[k]
        halves.append(total)
    return halves


def eliminate(tiles, count, first):
    shape_of = tiles[0].shape
    index = iota(shape_of, 0)
    for base in range(0, count, 4):
        columns = [
            jnp.broadcast_to(tiles[0][:, first + base + a : first + base + a + 1], shape_of) for a in range(4)
        ]
        rows = [[tile[base + a : base + a + 1] for tile in tiles] for a in range(4)]
        factors = []
        done = []
        for a in range(4):
            pivot = columns[a][base + a : base + a + 1]
            inverse = 1.0 / pivot
            for c in range(a + 1, 4):
                lower = columns[a][base + c : base + c + 1] * inverse
                upper = columns[c][base + a : base + a + 1] * inverse
                rows[c] = [row - lower * top for row, top in zip(rows[c], rows[a])]
                columns[c] = columns[c] - columns[a] * upper
            factors.append(jnp.where(index >= base + 4, columns[a] * inverse, 0.0))
            root = jnp.sqrt(pivot)
            done.append([row / root for row in rows[a]])
        tiles = list(tiles)
        for i in range(len(tiles)):
            tile = tiles[i]
            for a in range(4):
                tile = tile - factors[a] * rows[a][i]
            for a in range(4):
                tile = jnp.where(index == base + a, done[a][i], tile)
            tiles[i] = tile
    return tiles


def pad_lanes(a, width=EDGE):
    return jnp.concatenate([a, jnp.zeros((a.shape[0], width - a.shape[1]), F32)], axis=1)


def inverse_factor(square):
    both = pad_lanes(jnp.concatenate([square, eye(BLK, F32)], axis=1))
    return eliminate([both], BLK, 0)[0][:, BLK : 2 * BLK]


def first_solve_body(
    nodes, got_ref, all_ref, scale_ref, first_ref, send_ref, own_ref, next_ref, gram_ref, inv_ref
):
    top, bottom = sum_halves(got_ref)
    mine = jnp.concatenate([top[BLK:], bottom[BLK:]], axis=0)
    low = jnp.concatenate(
        [top[:BLK], pltpu.roll(mine, BLK, 1), pltpu.roll(mine, EDGE - BLK, 1), bottom[:BLK]], axis=0
    )
    row, lane = iota((EDGE, EDGE), 0), iota((EDGE, EDGE), 1)
    inner_row = (row >= BLK) & (row < 3 * BLK)
    inner_lane = (lane >= BLK) & (lane < 3 * BLK)
    gram = jnp.where(inner_row & jnp.logical_not(inner_lane), low.T, low)
    gram_ref[...] = gram
    unit = jnp.where(row[BLK:] == lane[BLK:], 1.0, 0.0)
    lower = eliminate([gram[BLK:], unit], 3 * BLK, BLK)[1]
    lower = jnp.concatenate([jnp.zeros((BLK, EDGE), F32), lower], axis=0)
    inv = dot_exact(lower.T, lower)
    inv_ref[...] = inv
    coef = dot_exact(gram[:BLK], inv)
    mix = jnp.where(lane[:BLK] < BLK, jnp.where(row[:BLK] == lane[:BLK], 1.0, 0.0), -coef).astype(BF16)
    wide = mix.astype(F32)
    squares = dot_exact(dot_exact(wide, gram), wide, NT) / nodes
    factor = inverse_factor(squares)
    remainder = dot(mix, all_ref[...])
    new = dot_exact(factor, remainder).astype(BF16)
    first_ref[...] = new
    next_ref[...] = jnp.concatenate([new, all_ref[BLK:]], axis=0)
    spread(new, scale_ref[...], send_ref, own_ref)


def second_solve_body(nodes, got_ref, image_ref, basis_ref, gram_ref, inv_ref, second_ref):
    top, bottom = sum_halves(got_ref)
    cross, fresh = top[:BLK], bottom[:BLK]
    square = jnp.concatenate([top[BLK:, BLK * i : BLK * (i + 1)] for i in range(4)], axis=0)
    row, lane = iota((EDGE, EDGE), 0), iota((EDGE, EDGE), 1)
    inv = inv_ref[...]
    reach = dot_exact(fresh, inv)
    schur = fresh[:, :BLK] - dot_exact(reach, fresh, NT)
    lower = inverse_factor(schur)
    newest = dot_exact(dot_exact(cross[:, :BLK] - dot_exact(cross, reach, NT), lower, NT), lower)
    older = dot_exact(cross, inv) - dot_exact(newest, reach)
    coef = jnp.where(lane[:BLK] < BLK, pad_lanes(newest), older).astype(BF16)
    wide = coef.astype(F32)
    full = jnp.concatenate([fresh, jnp.zeros((3 * BLK, EDGE), F32)], axis=0)
    gram = jnp.where(row < BLK, full, jnp.where(lane < BLK, full.T, gram_ref[...]))
    mixed = dot_exact(wide, cross, NT)
    squares = (square - mixed - mixed.T + dot_exact(dot_exact(wide, gram), wide, NT)) / nodes
    factor = inverse_factor(squares)
    remainder = image_ref[...].astype(F32) - dot(coef, basis_ref[...])
    second_ref[...] = dot_exact(factor, remainder).astype(BF16)


def per_device(tiles, tile_rows, tile_cols, node_level, level_scale, stored_basis, start_block):
    tile_stack = tiles.reshape(tiles.shape[2:])
    side = lax.axis_size("row")
    held = stored_basis.shape[0]
    nodes = held * side * lax.axis_size("col")
    pieces = held // EDGE
    me = lax.axis_index("col").reshape(1)
    send_shape = shape((side, pieces, BLK, EDGE), BF16)
    own_shape = shape((pieces, BLK, EDGE), BF16)

    def product(send, own):
        col_blk = arrive(lax.all_to_all(send, "row", 0, 0).reshape(-1, BLK, EDGE))
        near, far = gather_col(own)
        bwd, keep, away = tile_pass(pieces, me, tile_rows, tile_cols, tile_stack, col_blk, near, far)
        bwd = lax.all_to_all(bwd.reshape(send.shape), "row", 0, 0)
        keep, fwd = scatter_col(keep, away)
        return keep, fwd, bwd

    send, own, scale, basis = prep(
        send_shape,
        own_shape,
        start_block.T,
        stored_basis.T,
        node_level.reshape(1, -1),
        level_scale.reshape(1, -1),
    )
    parts = product(send, own)
    every, keep, away = image_call(
        first_image_body, shape((EDGE, held), BF16), 3 * BLK // 2, me, (*parts, own, scale, basis)
    )
    got = reduce_all(keep, away)
    square_shape = shape((EDGE, EDGE), F32)
    first, send, own, basis, gram, inv = call(
        lambda *refs: first_solve_body(nodes, *refs),
        (
            shape((BLK, held), BF16),
            send_shape,
            own_shape,
            shape((EDGE, held), BF16),
            square_shape,
            square_shape,
        ),
        (got, every, scale),
    )
    parts = product(send, own)
    image, keep, away = image_call(
        second_image_body, shape((BLK, held), BF16), BLK + 8, me, (*parts, own, scale, basis)
    )
    got = reduce_all(keep, away)
    second = call(
        lambda *refs: second_solve_body(nodes, *refs),
        shape((BLK, held), BF16),
        (got, image, basis, gram, inv),
    )
    return (first.T, second.T)


def solution(mesh):
    return jax.shard_map(
        per_device,
        mesh=mesh,
        in_specs=(
            P("row", "col", None, None, None),
            P("row", "col", None),
            P("row", "col", None),
            P(("row", "col")),
            P(),
            P(("row", "col"), None),
            P(("row", "col"), None),
        ),
        out_specs=(P(("row", "col"), None), P(("row", "col"), None)),
        check_vma=False,
    )
```

time: 300 us -> 201 us (0.67)
  blocking collectives: 194 us -> 67.9 us
  starting transfers between devices: 14.4 us -> 50.3 us
  Pallas kernels: 49 us -> 29.8 us
  waiting for transfers between devices: 28.3 us -> 46.7 us
  local copies, waits for them, and re-layouts: 8.58 us -> 1.62 us
    all_to_all x10 -> x4, blocking collectives: 194 us -> 67.9 us  [the longest x2 40.2 us: reduce_all(): lax.all_to_all(call(repeat_body, out, (keep, swap(send, 1))), 'row', 0, 0)]
    ppermute x0 -> x22, waiting for transfers between devices: none -> 36 us  [swap(): lax.ppermute(a, 'col', [(i, i ^ mask) for i in range(lax.axis_size('col'))])]
    ppermute x0 -> x22, starting transfers between devices: none -> 26 us  [swap(): lax.ppermute(a, 'col', [(i, i ^ mask) for i in range(lax.axis_size('col'))])]
    all_to_all x2 -> x4, waiting for transfers between devices: 28.3 us -> 10.7 us  [the longest x2 7.22 us: product(): col_blk = arrive(lax.all_to_all(send, 'row', 0, 0).reshape(-1, BLK, EDGE))]
    pallas_call x7 -> x10, Pallas kernels: 25.3 us -> 10.9 us  [call(): pl.pallas_call(body, out_shape=out_shape, in_specs=whole(len(args)), out_...]
    all_to_all x2 -> x4, starting transfers between devices: 14.4 us -> 24.4 us  [the longest x2 12.8 us: product(): col_blk = arrive(lax.all_to_all(send, 'row', 0, 0).reshape(-1, BLK, EDGE))]
    unnamed x16, local copies, waits for them, and re-layouts: 8.58 us -> 1.56 us
    pallas_call x2 -> x7, Pallas kernels: 23.7 us -> 18.9 us  [the longest x2 16.5 us: tile_pass(): pl.pallas_call(lambda *refs: tile_body(pieces, *refs), out_shape=(shape(a...]
  transfers between devices with their start and end apart: 2 -> 26, of which waited for: 2 -> 20; matrix products, arithmetic and copies ran while one was open for 1% -> 0% of each run, Pallas kernels for 0% -> 0%
where the time goes in v2:
time: 201 us; the launch traced here: 197 us
  blocking collectives  67.9 us (34%)
  starting transfers between devices  50.3 us (25%)
  waiting for transfers between devices  46.7 us (23%)
  Pallas kernels  29.8 us (15%)
    all_to_all x2, blocking collectives, reduce_all(): lax.all_to_all(call(repeat_body, out, (keep, swap(send, 1))), 'row', 0, 0)  40.2 us
    ppermute x22, waiting for transfers between devices, swap(): lax.ppermute(a, 'col', [(i, i ^ mask) for i in range(lax.axis_size('col'))])  36 us
    all_to_all x2, blocking collectives, reduce_all(): return lax.all_to_all(call(repeat_body, out, (got,)), 'col', 0, 0)  27.7 us
    ppermute x22, starting transfers between devices, swap(): lax.ppermute(a, 'col', [(i, i ^ mask) for i in range(lax.axis_size('col'))])  26 us
    pallas_call x2, Pallas kernels, tile_pass(): pl.pallas_call(lambda *refs: tile_body(pieces, *refs), out_shape=(shape(a...  16.5 us
    all_to_all x2, starting transfers between devices, product(): col_blk = arrive(lax.all_to_all(send, 'row', 0, 0).reshape(-1, BLK, EDGE))  12.8 us
    all_to_all x2, starting transfers between devices, product(): bwd = lax.all_to_all(bwd.reshape(send.shape), 'row', 0, 0)  11.6 us
    pallas_call x10, Pallas kernels, call(): pl.pallas_call(body, out_shape=out_shape, in_specs=whole(len(args)), out_...  10.9 us
  transfers between devices with their start and end apart: 26, of which 20 were waited for; matrix products, arithmetic and copies ran while one was open for 0% of the time, Pallas kernels for 0%

profile of v2, /device:TPU:4, one launch (start us, length us, event | category | flops | bytes accessed | tf_op | source)
XLA Modules:
  0.0 197.2 jit_solution(15951484761768091960)
XLA Ops:
  0.6 1.9 shard_map.86
  2.5 9.2 %all-to-all-start = ((bf16[16,4,32,128]{3,2,1,0:T(8,128)(2,1)}), bf16[16,4,32,128]{3,2,1,0:T(8,128)(2,1)S(1)}, u32[]{:S(2)}, u32[]{:S(2)}) async-start(bf16[16,4,32,128]{3,2,1,0:T(8,128)(2,1)} %get-tuple-element.36), calls=%async_computation | async-start | bytes 1048576 | tf_op jit(solution)/shard_map/all_to_all | solution.py:434
  13.5 4.0 %collective-permute-done = bf16[4,32,128]{2,1,0:T(8,128)(2,1)S(1)} collective-permute-done((bf16[4,32,128]{2,1,0:T(8,128)(2,1)}, bf16[4,32,128]{2,1,0:T(8,128)(2,1)S(1)}, u32[]{:S(2)}, u32[]{:S(2)}) %collective-permute-start) | collective-permute-done | bytes 32800 | tf_op jit(solution)/shard_map/ppermute | solution.py:217
  17.5 1.7 collective-permute-start.1
  19.2 2.2 %collective-permute-start.3 = (bf16[8,32,128]{2,1,0:T(8,128)(2,1)S(1)}, bf16[8,32,128]{2,1,0:T(8,128)(2,1)S(1)}, u32[]{:S(2)}, u32[]{:S(2)}) collective-permute-start(bf16[8,32,128]{2,1,0:T(8,128)(2,1)S(1)} %get-tuple-element.74), channel_id=1, source_target_pairs={{0,12},{1,13},{2,14},{3,15},{4,8},{5,9},{6,10},{7,11},{8,4},{9,5},... | collective-permute-start | bytes 196616 | tf_op jit(solution)/shard_map/ppermute | solution.py:217
  22.1 5.0 %collective-permute-done.2 = bf16[8,32,128]{2,1,0:T(8,128)(2,1)S(1)} collective-permute-done((bf16[8,32,128]{2,1,0:T(8,128)(2,1)S(1)}, bf16[8,32,128]{2,1,0:T(8,128)(2,1)S(1)}, u32[]{:S(2)}, u32[]{:S(2)}) %collective-permute-start.2) | collective-permute-done | bytes 65568 | tf_op jit(solution)/shard_map/ppermute | solution.py:217
  29.6 8.2 %shard_map.88 = (bf16[64,32,128]{2,1,0:T(8,128)(2,1)}, bf16[32,32,128]{2,1,0:T(8,128)(2,1)S(1)}, bf16[32,32,128]{2,1,0:T(8,128)(2,1)S(1)}) custom-call(s32[1]{0:T(128)} %bitcast.refs_0_.core_ref, s32[1,1,320]{2,1,0:T(1,128)S(1)} %copy-done.3, s32[1,1,320]{2,1,0:T(1,128)S(1)} %copy-done.4, bf16[320,128,128]{2,1,0:T(8,128)(2,1)} %bitcast.19, ...), custom_call_target="tpu_custom_call" | custom-call | flops 8000000000 | bytes 14000000 | tf_op jit(solution)/shard_map/pallas_call | solution.py:178
  37.9 7.2 %all-to-all-start.1 = ((bf16[16,4,32,128]{3,2,1,0:T(8,128)(2,1)}), bf16[16,4,32,128]{3,2,1,0:T(8,128)(2,1)S(1)}, u32[]{:S(2)}, u32[]{:S(2)}) async-start(bf16[16,4,32,128]{3,2,1,0:T(8,128)(2,1)} %bitcast.7), calls=%async_computation.1 | async-start | bytes 1048576 | tf_op jit(solution)/shard_map/all_to_all | solution.py:437
  47.6 1.8 collective-permute-start.7
  49.4 2.2 %collective-permute-start.8 = (bf16[8,32,128]{2,1,0:T(8,128)(2,1)S(1)}, bf16[8,32,128]{2,1,0:T(8,128)(2,1)S(1)}, u32[]{:S(2)}, u32[]{:S(2)}) collective-permute-start(bf16[8,32,128]{2,1,0:T(8,128)(2,1)S(1)} %get-tuple-element.43), channel_id=1, source_target_pairs={{0,12},{1,13},{2,14},{3,15},{4,8},{5,9},{6,10},{7,11},{8,4},{9,5},... | collective-permute-start | bytes 196616 | tf_op jit(solution)/shard_map/ppermute | solution.py:217
  51.7 1.7 collective-permute-done.7.refs_2_
  56.0 4.6 %collective-permute-done.9.fwd_ref = bf16[4,32,128]{2,1,0:T(8,128)(2,1)S(1)} collective-permute-done((bf16[4,32,128]{2,1,0:T(8,128)(2,1)S(1)}, bf16[4,32,128]{2,1,0:T(8,128)(2,1)S(1)}, u32[]{:S(2)}, u32[]{:S(2)}) %collective-permute-start.9) | collective-permute-done | bytes 32800 | tf_op jit(solution)/shard_map/ppermute | solution.py:217
  60.6 2.4 %all-to-all-done.1.bwd_ref = bf16[16,4,32,128]{3,2,1,0:T(8,128)(2,1)S(1)} async-done(((bf16[16,4,32,128]{3,2,1,0:T(8,128)(2,1)}), bf16[16,4,32,128]{3,2,1,0:T(8,128)(2,1)S(1)}, u32[]{:S(2)}, u32[]{:S(2)}) %all-to-all-start.1) | async-done | bytes 524320 | tf_op jit(solution)/shard_map/all_to_all | solution.py:437
  64.6 20.3 %all_to_all.40.refs_0_ = f32[16,48,128]{2,1,0:T(8,128)S(1)} all-to-all(f32[16,48,128]{2,1,0:T(8,128)S(1)} %shard_map.92), channel_id=1, replica_groups=mesh['row'=16,'col'=16] {'row'}, dimensions={0} | all-to-all | bytes 786432 | tf_op jit(solution)/shard_map/all_to_all | solution.py:316
  84.9 14.6 %all_to_all.41.refs_0_ = f32[16,48,128]{2,1,0:T(8,128)S(1)} all-to-all(f32[16,48,128]{2,1,0:T(8,128)S(1)} %shard_map.93), channel_id=1, replica_groups=mesh['row'=16,'col'=16] {'col'}, dimensions={0} | all-to-all | bytes 786432 | tf_op jit(solution)/shard_map/all_to_all | solution.py:317
  99.5 6.4 %shard_map.94 = (bf16[32,512]{1,0:T(8,128)(2,1)}, bf16[16,4,32,128]{3,2,1,0:T(8,128)(2,1)}, bf16[4,32,128]{2,1,0:T(8,128)(2,1)S(1)}, bf16[128,512]{1,0:T(8,128)(...) custom-call(f32[16,48,128]{2,1,0:T(8,128)S(1)} %all_to_all.41.refs_0_, ...), custom_call_target="tpu_custom_call" | custom-call | tf_op jit(solution)/shard_map/pallas_call | solution.py:41
  105.9 3.6 %all-to-all-start.4 = ((bf16[16,4,32,128]{3,2,1,0:T(8,128)(2,1)}), bf16[16,4,32,128]{3,2,1,0:T(8,128)(2,1)S(1)}, u32[]{:S(2)}, u32[]{:S(2)}) async-start(bf16[16,4,32,128]{3,2,1,0:T(8,128)(2,1)} %get-tuple-element.53), calls=%async_computation.4 | async-start | bytes 1048576 | tf_op jit(solution)/shard_map/all_to_all | solution.py:434
  109.4 2.8 %collective-permute-start.11 = (bf16[4,32,128]{2,1,0:T(8,128)(2,1)S(1)}, bf16[4,32,128]{2,1,0:T(8,128)(2,1)S(1)}, u32[]{:S(2)}, u32[]{:S(2)}) collective-permute-start(bf16[4,32,128]{2,1,0:T(8,128)(2,1)S(1)} %get-tuple-element.54.own_ref), channel_id=1, source_target_pairs={{0,2},{1,3},{2,0},{3,1},{4,6},{5,7},{6,4},{7,5},{8,10},{9,11},{10,... | collective-permute-start | bytes 98312 | tf_op jit(solution)/shard_map/ppermute | solution.py:217
  112.3 2.7 %collective-permute-done.11 = bf16[4,32,128]{2,1,0:T(8,128)(2,1)S(1)} collective-permute-done((bf16[4,32,128]{2,1,0:T(8,128)(2,1)S(1)}, bf16[4,32,128]{2,1,0:T(8,128)(2,1)S(1)}, u32[]{:S(2)}, u32[]{:S(2)}) %collective-permute-start.11) | collective-permute-done | bytes 32800 | tf_op jit(solution)/shard_map/ppermute | solution.py:217
  116.4 2.8 %collective-permute-start.13 = (bf16[8,32,128]{2,1,0:T(8,128)(2,1)S(1)}, bf16[8,32,128]{2,1,0:T(8,128)(2,1)S(1)}, u32[]{:S(2)}, u32[]{:S(2)}) collective-permute-start(bf16[8,32,128]{2,1,0:T(8,128)(2,1)S(1)} %get-tuple-element.70), channel_id=1, source_target_pairs={{0,8},{1,9},{2,10},{3,11},{4,12},{5,13},{6,14},{7,15},{8,0},{9,1},... | collective-permute-start | bytes 196616 | tf_op jit(solution)/shard_map/ppermute | solution.py:217
  119.9 2.3 %collective-permute-done.13 = bf16[8,32,128]{2,1,0:T(8,128)(2,1)S(1)} collective-permute-done((bf16[8,32,128]{2,1,0:T(8,128)(2,1)S(1)}, bf16[8,32,128]{2,1,0:T(8,128)(2,1)S(1)}, u32[]{:S(2)}, u32[]{:S(2)}) %collective-permute-start.13) | collective-permute-done | bytes 65568 | tf_op jit(solution)/shard_map/ppermute | solution.py:217
  122.3 5.6 %all-to-all-done.4 = bf16[16,4,32,128]{3,2,1,0:T(8,128)(2,1)S(1)} async-done(((bf16[16,4,32,128]{3,2,1,0:T(8,128)(2,1)}), bf16[16,4,32,128]{3,2,1,0:T(8,128)(2,1)S(1)}, u32[]{:S(2)}, u32[]{:S(2)}) %all-to-all-start.4) | async-done | bytes 524320 | tf_op jit(solution)/shard_map/all_to_all | solution.py:434
  127.9 8.2 %shard_map.96 = (bf16[64,32,128]{2,1,0:T(8,128)(2,1)}, bf16[32,32,128]{2,1,0:T(8,128)(2,1)S(1)}, bf16[32,32,128]{2,1,0:T(8,128)(2,1)S(1)}) custom-call(s32[1]{0:T(128)} %bitcast.refs_0_.core_ref, s32[1,1,320]{2,1,0:T(1,128)S(1)} %copy-done.3, s32[1,1,320]{2,1,0:T(1,128)S(1)} %copy-done.4, bf16[320,128,128]{2,1,0:T(8,128)(2,1)} %bitcast.20, ...), custom_call_target="tpu_custom_call" | custom-call | flops 8000000000 | bytes 14000000 | tf_op jit(solution)/shard_map/pallas_call | solution.py:178
  136.1 4.3 %all-to-all-start.5 = ((bf16[16,4,32,128]{3,2,1,0:T(8,128)(2,1)}), bf16[16,4,32,128]{3,2,1,0:T(8,128)(2,1)S(1)}, u32[]{:S(2)}, u32[]{:S(2)}) async-start(bf16[16,4,32,128]{3,2,1,0:T(8,128)(2,1)} %bitcast.10), calls=%async_computation.5 | async-start | bytes 1048576 | tf_op jit(solution)/shard_map/all_to_all | solution.py:437
  143.3 2.5 %collective-permute-start.18 = (bf16[8,32,128]{2,1,0:T(8,128)(2,1)S(1)}, bf16[8,32,128]{2,1,0:T(8,128)(2,1)S(1)}, u32[]{:S(2)}, u32[]{:S(2)}) collective-permute-start(bf16[8,32,128]{2,1,0:T(8,128)(2,1)S(1)} %get-tuple-element.59), channel_id=1, source_target_pairs={{0,8},{1,9},{2,10},{3,11},{4,12},{5,13},{6,14},{7,15},{8,0},{9,1},... | collective-permute-start | bytes 196616 | tf_op jit(solution)/shard_map/ppermute | solution.py:217
  147.0 2.4 %collective-permute-done.18.refs_2_ = bf16[8,32,128]{2,1,0:T(8,128)(2,1)S(1)} collective-permute-done((bf16[8,32,128]{2,1,0:T(8,128)(2,1)S(1)}, bf16[8,32,128]{2,1,0:T(8,128)(2,1)S(1)}, u32[]{:S(2)}, u32[]{:S(2)}) %collective-permute-start.18) | collective-permute-done | bytes 65568 | tf_op jit(solution)/shard_map/ppermute | solution.py:217
  149.4 1.9 collective-permute-done.19.refs_3_
  151.4 2.3 %collective-permute-start.20 = (bf16[4,32,128]{2,1,0:T(8,128)(2,1)S(1)}, bf16[4,32,128]{2,1,0:T(8,128)(2,1)S(1)}, u32[]{:S(2)}, u32[]{:S(2)}) collective-permute-start(bf16[4,32,128]{2,1,0:T(8,128)(2,1)S(1)} %get-tuple-element.62), channel_id=1, source_target_pairs={{0,2},{1,3},{2,0},{3,1},{4,6},{5,7},{6,4},{7,5},{8,10},{9,11},{10,... | collective-permute-start | bytes 98312 | tf_op jit(solution)/shard_map/ppermute | solution.py:217
  153.7 3.6 %collective-permute-done.20.fwd_ref = bf16[4,32,128]{2,1,0:T(8,128)(2,1)S(1)} collective-permute-done((bf16[4,32,128]{2,1,0:T(8,128)(2,1)S(1)}, bf16[4,32,128]{2,1,0:T(8,128)(2,1)S(1)}, u32[]{:S(2)}, u32[]{:S(2)}) %collective-permute-start.20) | collective-permute-done | bytes 32800 | tf_op jit(solution)/shard_map/ppermute | solution.py:217
  159.9 19.9 %all_to_all.42.refs_0_ = f32[16,40,128]{2,1,0:T(8,128)S(1)} all-to-all(f32[16,40,128]{2,1,0:T(8,128)S(1)} %shard_map.100), channel_id=1, replica_groups=mesh['row'=16,'col'=16] {'row'}, dimensions={0} | all-to-all | bytes 655360 | tf_op jit(solution)/shard_map/all_to_all | solution.py:316
  179.9 13.1 %all_to_all.43.refs_0_ = f32[16,40,128]{2,1,0:T(8,128)S(1)} all-to-all(f32[16,40,128]{2,1,0:T(8,128)S(1)} %shard_map.101), channel_id=1, replica_groups=mesh['row'=16,'col'=16] {'col'}, dimensions={0} | all-to-all | bytes 655360 | tf_op jit(solution)/shard_map/all_to_all | solution.py:317
  193.0 4.2 %shard_map.102 = bf16[32,512]{1,0:T(8,128)(2,1)} custom-call(f32[16,40,128]{2,1,0:T(8,128)S(1)} %all_to_all.43.refs_0_, bf16[32,512]{1,0:T(8,128)(2,1)S(1)} %get-tuple-element.67.refs_1_, bf16[128,512]{1,0:T(8,128)(2,1)S(1)} %get-tuple-element.64.basis_ref.refs_2_, f32[128,128]{1,0:T(8,128)S(1)} %get-tuple-element.68.refs_3_, ...), custom_call_target="tpu_custom_call" | custom-call | tf_op jit(solution)/shard_map/pallas_call | solution.py:41
  (61 shorter events, 20.8 us)
Async XLA Ops:
  2.5 26.4 %all-to-all-start = ((bf16[16,4,32,128]{3,2,1,0:T(8,128)(2,1)}), bf16[16,4,32,128]{3,2,1,0:T(8,128)(2,1)S(1)}, u32[]{:S(2)}, u32[]{:S(2)}) async-start(bf16[16,4,32,128]{3,2,1,0:T(8,128)(2,1)} %get-tuple-element.36), calls=%async_computation | async-start | bytes 1048576 | tf_op jit(solution)/shard_map/all_to_all | solution.py:434
  11.8 5.7 %collective-permute-start = (bf16[4,32,128]{2,1,0:T(8,128)(2,1)}, bf16[4,32,128]{2,1,0:T(8,128)(2,1)S(1)}, u32[]{:S(2)}, u32[]{:S(2)}) collective-permute-start(bf16[4,32,128]{2,1,0:T(8,128)(2,1)} %get-tuple-element.37.own_ref), channel_id=1, source_target_pairs={{0,2},{1,3},{2,0},{3,1},{4,6},{5,7},{6,4},{7,5},{8,10},{9,11},{10,... | collective-permute-start | bytes 98312 | tf_op jit(solution)/shard_map/ppermute | solution.py:217
  17.5 4.6 %collective-permute-start.1 = (bf16[8,32,128]{2,1,0:T(8,128)(2,1)S(1)}, bf16[8,32,128]{2,1,0:T(8,128)(2,1)S(1)}, u32[]{:S(2)}, u32[]{:S(2)}) collective-permute-start(bf16[8,32,128]{2,1,0:T(8,128)(2,1)S(1)} %get-tuple-element.74), channel_id=1, source_target_pairs={{0,4},{1,5},{2,6},{3,7},{4,0},{5,1},{6,2},{7,3},{8,12},{9,13},{10,... | collective-permute-start | bytes 196616 | tf_op jit(solution)/shard_map/ppermute | solution.py:217
  19.2 8.0 %collective-permute-start.3 = (bf16[8,32,128]{2,1,0:T(8,128)(2,1)S(1)}, bf16[8,32,128]{2,1,0:T(8,128)(2,1)S(1)}, u32[]{:S(2)}, u32[]{:S(2)}) collective-permute-start(bf16[8,32,128]{2,1,0:T(8,128)(2,1)S(1)} %get-tuple-element.74), channel_id=1, source_target_pairs={{0,12},{1,13},{2,14},{3,15},{4,8},{5,9},{6,10},{7,11},{8,4},{9,5},... | collective-permute-start | bytes 196616 | tf_op jit(solution)/shard_map/ppermute | solution.py:217
  21.4 5.8 %collective-permute-start.2 = (bf16[8,32,128]{2,1,0:T(8,128)(2,1)S(1)}, bf16[8,32,128]{2,1,0:T(8,128)(2,1)S(1)}, u32[]{:S(2)}, u32[]{:S(2)}) collective-permute-start(bf16[8,32,128]{2,1,0:T(8,128)(2,1)S(1)} %get-tuple-element.74), channel_id=1, source_target_pairs={{0,8},{1,9},{2,10},{3,11},{4,12},{5,13},{6,14},{7,15},{8,0},{9,1},... | collective-permute-start | bytes 196616 | tf_op jit(solution)/shard_map/ppermute | solution.py:217
  27.2 1.8 collective-permute-start.4
  28.9 0.7 copy-start.3
  28.9 0.7 copy-start.4
  29.6 33.4 %copy-start = (bf16[4,32,128]{2,1,0:T(8,128)(2,1)S(1)}, bf16[4,32,128]{2,1,0:T(8,128)(2,1)}, u32[]{:S(2)}) copy-start(bf16[4,32,128]{2,1,0:T(8,128)(2,1)} %get-tuple-element.37.own_ref) | copy-start | bytes 98308
  29.6 33.4 %copy-start.1 = (bf16[96,512]{1,0:T(8,128)(2,1)S(1)}, bf16[96,512]{1,0:T(8,128)(2,1)}, u32[]{:S(2)}) copy-start(bf16[96,512]{1,0:T(8,128)(2,1)} %get-tuple-element.48.basis_ref) | copy-start | bytes 294916
  29.6 33.4 %copy-start.2 = (f32[1,512]{1,0:T(1,128)S(1)}, f32[1,512]{1,0:T(1,128)}, u32[]{:S(2)}) copy-start(f32[1,512]{1,0:T(1,128)} %get-tuple-element.47.scale_ref.refs_2_) | copy-start | bytes 6148
  37.9 25.1 %all-to-all-start.1 = ((bf16[16,4,32,128]{3,2,1,0:T(8,128)(2,1)}), bf16[16,4,32,128]{3,2,1,0:T(8,128)(2,1)S(1)}, u32[]{:S(2)}, u32[]{:S(2)}) async-start(bf16[16,4,32,128]{3,2,1,0:T(8,128)(2,1)} %bitcast.7), calls=%async_computation.1 | async-start | bytes 1048576 | tf_op jit(solution)/shard_map/all_to_all | solution.py:437
  45.1 1.6 collective-permute-start.5
  46.8 4.9 %collective-permute-start.6 = (bf16[8,32,128]{2,1,0:T(8,128)(2,1)S(1)}, bf16[8,32,128]{2,1,0:T(8,128)(2,1)S(1)}, u32[]{:S(2)}, u32[]{:S(2)}) collective-permute-start(bf16[8,32,128]{2,1,0:T(8,128)(2,1)S(1)} %get-tuple-element.41), channel_id=1, source_target_pairs={{0,4},{1,5},{2,6},{3,7},{4,0},{5,1},{6,2},{7,3},{8,12},{9,13},{10,... | collective-permute-start | bytes 196616 | tf_op jit(solution)/shard_map/ppermute | solution.py:217
  47.6 5.8 %collective-permute-start.7 = (bf16[8,32,128]{2,1,0:T(8,128)(2,1)S(1)}, bf16[8,32,128]{2,1,0:T(8,128)(2,1)S(1)}, u32[]{:S(2)}, u32[]{:S(2)}) collective-permute-start(bf16[8,32,128]{2,1,0:T(8,128)(2,1)S(1)} %get-tuple-element.42), channel_id=1, source_target_pairs={{0,8},{1,9},{2,10},{3,11},{4,12},{5,13},{6,14},{7,15},{8,0},{9,1},... | collective-permute-start | bytes 196616 | tf_op jit(solution)/shard_map/ppermute | solution.py:217
  49.4 5.5 %collective-permute-start.8 = (bf16[8,32,128]{2,1,0:T(8,128)(2,1)S(1)}, bf16[8,32,128]{2,1,0:T(8,128)(2,1)S(1)}, u32[]{:S(2)}, u32[]{:S(2)}) collective-permute-start(bf16[8,32,128]{2,1,0:T(8,128)(2,1)S(1)} %get-tuple-element.43), channel_id=1, source_target_pairs={{0,12},{1,13},{2,14},{3,15},{4,8},{5,9},{6,10},{7,11},{8,4},{9,5},... | collective-permute-start | bytes 196616 | tf_op jit(solution)/shard_map/ppermute | solution.py:217
  54.9 5.7 %collective-permute-start.9 = (bf16[4,32,128]{2,1,0:T(8,128)(2,1)S(1)}, bf16[4,32,128]{2,1,0:T(8,128)(2,1)S(1)}, u32[]{:S(2)}, u32[]{:S(2)}) collective-permute-start(bf16[4,32,128]{2,1,0:T(8,128)(2,1)S(1)} %get-tuple-element.45), channel_id=1, source_target_pairs={{0,2},{1,3},{2,0},{3,1},{4,6},{5,7},{6,4},{7,5},{8,10},{9,11},{10,... | collective-permute-start | bytes 98312 | tf_op jit(solution)/shard_map/ppermute | solution.py:217
  63.3 1.3 collective-permute-start.10
  105.9 22.0 %all-to-all-start.4 = ((bf16[16,4,32,128]{3,2,1,0:T(8,128)(2,1)}), bf16[16,4,32,128]{3,2,1,0:T(8,128)(2,1)S(1)}, u32[]{:S(2)}, u32[]{:S(2)}) async-start(bf16[16,4,32,128]{3,2,1,0:T(8,128)(2,1)} %get-tuple-element.53), calls=%async_computation.4 | async-start | bytes 1048576 | tf_op jit(solution)/shard_map/all_to_all | solution.py:434
  109.4 5.5 %collective-permute-start.11 = (bf16[4,32,128]{2,1,0:T(8,128)(2,1)S(1)}, bf16[4,32,128]{2,1,0:T(8,128)(2,1)S(1)}, u32[]{:S(2)}, u32[]{:S(2)}) collective-permute-start(bf16[4,32,128]{2,1,0:T(8,128)(2,1)S(1)} %get-tuple-element.54.own_ref), channel_id=1, source_target_pairs={{0,2},{1,3},{2,0},{3,1},{4,6},{5,7},{6,4},{7,5},{8,10},{9,11},{10,... | collective-permute-start | bytes 98312 | tf_op jit(solution)/shard_map/ppermute | solution.py:217
  115.0 4.9 %collective-permute-start.12 = (bf16[8,32,128]{2,1,0:T(8,128)(2,1)S(1)}, bf16[8,32,128]{2,1,0:T(8,128)(2,1)S(1)}, u32[]{:S(2)}, u32[]{:S(2)}) collective-permute-start(bf16[8,32,128]{2,1,0:T(8,128)(2,1)S(1)} %get-tuple-element.70), channel_id=1, source_target_pairs={{0,4},{1,5},{2,6},{3,7},{4,0},{5,1},{6,2},{7,3},{8,12},{9,13},{10,... | collective-permute-start | bytes 196616 | tf_op jit(solution)/shard_map/ppermute | solution.py:217
  115.1 7.1 %collective-permute-start.14 = (bf16[8,32,128]{2,1,0:T(8,128)(2,1)S(1)}, bf16[8,32,128]{2,1,0:T(8,128)(2,1)S(1)}, u32[]{:S(2)}, u32[]{:S(2)}) collective-permute-start(bf16[8,32,128]{2,1,0:T(8,128)(2,1)S(1)} %get-tuple-element.70), channel_id=1, source_target_pairs={{0,12},{1,13},{2,14},{3,15},{4,8},{5,9},{6,10},{7,11},{8,4},{9,5},... | collective-permute-start | bytes 196616 | tf_op jit(solution)/shard_map/ppermute | solution.py:217
  116.4 5.8 %collective-permute-start.13 = (bf16[8,32,128]{2,1,0:T(8,128)(2,1)S(1)}, bf16[8,32,128]{2,1,0:T(8,128)(2,1)S(1)}, u32[]{:S(2)}, u32[]{:S(2)}) collective-permute-start(bf16[8,32,128]{2,1,0:T(8,128)(2,1)S(1)} %get-tuple-element.70), channel_id=1, source_target_pairs={{0,8},{1,9},{2,10},{3,11},{4,12},{5,13},{6,14},{7,15},{8,0},{9,1},... | collective-permute-start | bytes 196616 | tf_op jit(solution)/shard_map/ppermute | solution.py:217
  122.2 5.7 %collective-permute-start.15 = (bf16[32,32,128]{2,1,0:T(8,128)(2,1)S(1)}, bf16[32,32,128]{2,1,0:T(8,128)(2,1)S(1)}, u32[]{:S(2)}, u32[]{:S(2)}) collective-permute-start(bf16[32,32,128]{2,1,0:T(8,128)(2,1)S(1)} %constant_dynamic-update-slice_fusion.9.refs_5_), channel_id=1, source_target_pairs={{0,1},{1,0},{2,3},{3,2},{4,5},{5,4},{6,7},{7,6},{8,9},{9,8},{10,11... | collective-permute-start | bytes 786440 | tf_op jit(solution)/shard_map/ppermute | solution.py:217
  136.1 22.2 %all-to-all-start.5 = ((bf16[16,4,32,128]{3,2,1,0:T(8,128)(2,1)}), bf16[16,4,32,128]{3,2,1,0:T(8,128)(2,1)S(1)}, u32[]{:S(2)}, u32[]{:S(2)}) async-start(bf16[16,4,32,128]{3,2,1,0:T(8,128)(2,1)} %bitcast.10), calls=%async_computation.5 | async-start | bytes 1048576 | tf_op jit(solution)/shard_map/all_to_all | solution.py:437
  140.5 1.6 collective-permute-start.16
  142.2 4.8 %collective-permute-start.17 = (bf16[8,32,128]{2,1,0:T(8,128)(2,1)S(1)}, bf16[8,32,128]{2,1,0:T(8,128)(2,1)S(1)}, u32[]{:S(2)}, u32[]{:S(2)}) collective-permute-start(bf16[8,32,128]{2,1,0:T(8,128)(2,1)S(1)} %get-tuple-element.58), channel_id=1, source_target_pairs={{0,4},{1,5},{2,6},{3,7},{4,0},{5,1},{6,2},{7,3},{8,12},{9,13},{10,... | collective-permute-start | bytes 196616 | tf_op jit(solution)/shard_map/ppermute | solution.py:217
  143.3 6.1 %collective-permute-start.18 = (bf16[8,32,128]{2,1,0:T(8,128)(2,1)S(1)}, bf16[8,32,128]{2,1,0:T(8,128)(2,1)S(1)}, u32[]{:S(2)}, u32[]{:S(2)}) collective-permute-start(bf16[8,32,128]{2,1,0:T(8,128)(2,1)S(1)} %get-tuple-element.59), channel_id=1, source_target_pairs={{0,8},{1,9},{2,10},{3,11},{4,12},{5,13},{6,14},{7,15},{8,0},{9,1},... | collective-permute-start | bytes 196616 | tf_op jit(solution)/shard_map/ppermute | solution.py:217
  145.8 5.5 %collective-permute-start.19 = (bf16[8,32,128]{2,1,0:T(8,128)(2,1)S(1)}, bf16[8,32,128]{2,1,0:T(8,128)(2,1)S(1)}, u32[]{:S(2)}, u32[]{:S(2)}) collective-permute-start(bf16[8,32,128]{2,1,0:T(8,128)(2,1)S(1)} %get-tuple-element.60), channel_id=1, source_target_pairs={{0,12},{1,13},{2,14},{3,15},{4,8},{5,9},{6,10},{7,11},{8,4},{9,5},... | collective-permute-start | bytes 196616 | tf_op jit(solution)/shard_map/ppermute | solution.py:217
  151.4 5.8 %collective-permute-start.20 = (bf16[4,32,128]{2,1,0:T(8,128)(2,1)S(1)}, bf16[4,32,128]{2,1,0:T(8,128)(2,1)S(1)}, u32[]{:S(2)}, u32[]{:S(2)}) collective-permute-start(bf16[4,32,128]{2,1,0:T(8,128)(2,1)S(1)} %get-tuple-element.62), channel_id=1, source_target_pairs={{0,2},{1,3},{2,0},{3,1},{4,6},{5,7},{6,4},{7,5},{8,10},{9,11},{10,... | collective-permute-start | bytes 98312 | tf_op jit(solution)/shard_map/ppermute | solution.py:217
  158.6 1.3 collective-permute-start.21
